TPU v7x, 512 devices: a whole 4x4x16 slice. The times are simulated.
512 devices in a mesh: dp: 16 (over y, x), ctx: 16 (over z), tp: 2 (over core).
Axes of the slice: x: 4, y: 4, z: 16, core: 2. Of those that a mesh axis runs over, the one named last changes fastest.
Arguments:
- q_proj: bfloat16 [16, 2048, 4096], P('dp', 'ctx', 'tp'), may hold values from -6 to 6
- q_bias: bfloat16 [4096], P('tp'), may hold values from -3 to 3
- k_proj: bfloat16 [16, 2048, 512], P('dp', 'ctx', 'tp'), may hold values from -6 to 6
- v_proj: bfloat16 [16, 2048, 512], P('dp', 'ctx', 'tp'), may hold values from -6 to 6
- v_bias: bfloat16 [512], P('tp'), may hold values from -3 to 3
- dout: bfloat16 [16, 2048, 4096], P('dp', 'ctx', 'tp'), may hold values from -6 to 6
- lengths: int32 [16, 8], P('dp'), may hold values from 1 to 1536, 2048 in all within a row
Outputs:
- attn_out: bfloat16 [16, 2048, 4096], P('dp', 'ctx', 'tp')
- q_grad: bfloat16 [16, 2048, 4096], P('dp', 'ctx', 'tp')
- k_grad: bfloat16 [16, 2048, 512], P('dp', 'ctx', 'tp')
- v_grad: bfloat16 [16, 2048, 512], P('dp', 'ctx', 'tp')
- q_bias_grad: float32 [4096], P('tp')
- v_bias_grad: float32 [512], P('tp')
All inputs are finite; a program needn't handle non-finite values.
Results may differ from a plain program's by a relative error of at most 0.035.
Values may be sent and summed in bfloat16 or wider, within the bound.
A program may use at most 64 MiB of HBM per device.

v0:
```python
import jax
import jax.numpy as jnp
from jax import lax
from jax.sharding import PartitionSpec as P

HEAD_DIM = 128
HEADS = 32
KV_HEADS = 4


def doc_index(positions, ends):
    return jnp.sum((positions[..., None] >= ends).astype(jnp.int32), axis=-1)


def shards(q_proj, q_bias, k_proj, v_proj, v_bias, dout, lengths):
    tok = q_proj.shape[1]
    half = tok // 2
    width = q_proj.shape[2]
    kv_width = k_proj.shape[2]
    kv_heads = kv_width // HEAD_DIM
    group = HEADS // KV_HEADS
    scale = HEAD_DIM ** (-0.5)
    ctx_size = lax.axis_size("ctx")
    ctx_rank = lax.axis_index("ctx")
    total_rows = tok * ctx_size
    queries = (q_proj[0].astype(jnp.float32) + q_bias.astype(jnp.float32)).astype(jnp.bfloat16)
    keys = k_proj[0]
    values = (v_proj[0].astype(jnp.float32) + v_bias.astype(jnp.float32)).astype(jnp.bfloat16)
    grads = dout[0]
    ends = jnp.cumsum(lengths[0])
    offsets = jnp.arange(half, dtype=jnp.int32)
    first_pos = ctx_rank * tok + offsets
    second_pos = ctx_rank * tok + half + offsets
    local_q = queries.reshape(2, half, width)
    local_g = grads.reshape(2, half, width)
    query_pos = jnp.stack([first_pos, second_pos])
    query_doc = doc_index(query_pos, ends)
    q_heads = local_q.reshape(2, half, kv_heads, group, HEAD_DIM)
    g_heads = local_g.reshape(2, half, kv_heads, group, HEAD_DIM).transpose(0, 2, 3, 1, 4)

    def live_of(index, key_pos, key_doc):
        return (key_pos[None, :] <= query_pos[index][:, None]) & (
            key_doc[None, :] == query_doc[index][:, None]
        )

    start_state = (
        jnp.full((2, kv_heads, group, half), -1e30, jnp.float32),
        jnp.zeros((2, kv_heads, group, half), jnp.float32),
        jnp.zeros((2, kv_heads, group, half, HEAD_DIM), jnp.float32),
    )
    block_k = lax.all_gather(keys, "ctx", axis=0, tiled=True)
    block_v = lax.all_gather(values, "ctx", axis=0, tiled=True)
    count = block_k.shape[0]
    key_pos = jnp.arange(count, dtype=jnp.int32)
    key_doc = doc_index(key_pos, ends)
    keys3 = block_k.reshape(count, kv_heads, HEAD_DIM)
    values3 = block_v.reshape(count, kv_heads, HEAD_DIM)
    updated = []
    for index in range(2):
        live = live_of(index, key_pos, key_doc)

        def attend(state, index=index, live=live):
            run_max, run_sum, run_acc = state
            score = (
                jnp.einsum(
                    "tkgd,skd->kgts", q_heads[index], keys3, preferred_element_type=jnp.float32
                )
                * scale
            )
            new_max = jnp.maximum(run_max, jnp.max(jnp.where(live, score, -1e30), axis=-1))
            weights = jnp.where(live, jnp.exp(score - new_max[..., None]), 0.0)
            run_sum = jnp.sum(weights, axis=-1)
            run_acc = jnp.einsum(
                "kgts,skd->kgtd",
                weights.astype(jnp.bfloat16),
                values3,
                preferred_element_type=jnp.float32,
            )
            return (new_max, run_sum, run_acc)

        state = (start_state[0][index], start_state[1][index], start_state[2][index])
        updated.append(lax.cond(jnp.any(live), attend, lambda st: st, state))
    run_max, run_sum, run_acc = tuple((jnp.stack([updated[0][n], updated[1][n]]) for n in range(3)))
    attn = (run_acc / run_sum[..., None]).astype(jnp.bfloat16)
    lse = run_max + jnp.log(run_sum)
    delta = jnp.sum(g_heads.astype(jnp.float32) * attn.astype(jnp.float32), axis=-1)
    q_start = jnp.zeros((2, kv_heads, group, half, HEAD_DIM), jnp.float32)
    q_acc = q_start
    block_k = lax.all_gather(keys, "ctx", axis=0, tiled=True)
    block_v = lax.all_gather(values, "ctx", axis=0, tiled=True)
    count = block_k.shape[0]
    key_pos = jnp.arange(count, dtype=jnp.int32)
    key_doc = doc_index(key_pos, ends)
    grad_keys3 = block_k.reshape(count, kv_heads, HEAD_DIM)
    grad_values3 = block_v.reshape(count, kv_heads, HEAD_DIM)
    key_term = jnp.zeros((count, kv_heads, HEAD_DIM), jnp.float32)
    value_term = jnp.zeros((count, kv_heads, HEAD_DIM), jnp.float32)
    new_q = []
    for index in range(2):
        live = live_of(index, key_pos, key_doc)

        def differentiate(state, index=index, live=live):
            q_part, k_part, v_part = state
            score = (
                jnp.einsum(
                    "tkgd,skd->kgts", q_heads[index], grad_keys3, preferred_element_type=jnp.float32
                )
                * scale
            )
            probs = jnp.where(live, jnp.exp(score - lse[index][..., None]), 0.0)
            v_part = v_part + jnp.einsum(
                "kgts,kgtd->skd",
                probs.astype(jnp.bfloat16),
                g_heads[index],
                preferred_element_type=jnp.float32,
            )
            dprob = jnp.einsum(
                "kgtd,skd->kgts", g_heads[index], grad_values3, preferred_element_type=jnp.float32
            )
            dscore = (probs * (dprob - delta[index][..., None])).astype(jnp.bfloat16)
            q_part = (
                jnp.einsum("kgts,skd->kgtd", dscore, grad_keys3, preferred_element_type=jnp.float32)
                * scale
            )
            k_part = (
                k_part
                + jnp.einsum(
                    "kgts,tkgd->skd", dscore, q_heads[index], preferred_element_type=jnp.float32
                )
                * scale
            )
            return (q_part, k_part, v_part)

        q_part, key_term, value_term = lax.cond(
            jnp.any(live), differentiate, lambda st: st, (q_acc[index], key_term, value_term)
        )
        new_q.append(q_part)
    q_acc = jnp.stack(new_q)
    term = jnp.stack([key_term, value_term], axis=1)
    kv_acc = term
    q_acc, kv_acc = (q_acc, kv_acc)
    shares = lax.psum_scatter(
        kv_acc.reshape(total_rows, 2 * kv_width).astype(jnp.bfloat16),
        "ctx",
        scatter_dimension=0,
        tiled=True,
    ).astype(jnp.float32)
    key_grad = shares[:, :kv_width].astype(jnp.bfloat16)
    value_full = shares[:, kv_width:]
    value_grad = value_full.astype(jnp.bfloat16)
    q_rows = q_acc.transpose(0, 3, 1, 2, 4).reshape(2, half, width)
    out_rows = attn.transpose(0, 3, 1, 2, 4).reshape(2, half, width)
    q_sum = jnp.sum(q_rows, axis=(0, 1))
    v_sum = jnp.sum(value_full, axis=0)
    q_rounded = q_rows.astype(jnp.bfloat16)
    attn_full = out_rows.reshape(tok, width)
    q_full = q_rounded.reshape(tok, width)
    totals = lax.psum((q_sum, v_sum), ("dp", "ctx"))
    batches = lax.axis_size("dp")
    return (
        attn_full[None],
        q_full[None],
        key_grad[None],
        value_grad[None],
        totals[0] / batches,
        totals[1] / batches,
    )


def solution(mesh):
    placed = (
        P("dp", "ctx", "tp"),
        P("tp"),
        P("dp", "ctx", "tp"),
        P("dp", "ctx", "tp"),
        P("tp"),
        P("dp", "ctx", "tp"),
        P("dp", None),
    )
    return jax.shard_map(
        shards,
        mesh=mesh,
        in_specs=placed,
        out_specs=(
            P("dp", "ctx", "tp"),
            P("dp", "ctx", "tp"),
            P("dp", "ctx", "tp"),
            P("dp", "ctx", "tp"),
            P("tp"),
            P("tp"),
        ),
        check_vma=False,
    )
```

profile of v0, /device:TPU:0, one launch (start us, length us, event | category | flops | bytes accessed | tf_op | source)
XLA Modules:
  0.0 999.7 jit_solution(1904077164591623939)
XLA Ops:
  17.9 64.1 %all-gather.6.cloned.1.call-done = bf16[1,2048,256]{1,2,0:T(8,128)(2,1)} async-done(((bf16[1,128,256]{1,2,0:T(8,128)(2,1)}), bf16[1,2048,256]{1,2,0:T(8,128)(2,1)}) %all-gather.6.cloned.1.call-update) | async-done | bytes 1048592 | tf_op jit(solution)/shard_map/all_gather | solution.py:51
  82.0 70.7 %all-gather.4.cloned.1.call-done = bf16[2048,256]{0,1:T(8,128)(2,1)} async-done(((bf16[128,256]{0,1:T(8,128)(2,1)}), bf16[2048,256]{0,1:T(8,128)(2,1)}) %all-gather.4.cloned.1.call-update) | async-done | bytes 1048592 | tf_op jit(solution)/shard_map/all_gather | solution.py:52
  152.7 7.3 conditional.4
  152.8 2.9 fusion
  157.4 2.3 fusion.4
  160.0 7.3 conditional.5
  160.2 2.9 fusion.17
  164.8 2.3 fusion.21
  168.9 13.7 %conditional.6 = (f32[2048,2,128]{2,0,1:T(8,128)S(1)}, f32[2048,2,128]{2,0,1:T(8,128)}, f32[1,2,8,64,128]{4,3,2,1,0:T(8,128)}) conditional(s32[]{:T(128)} %convert_element_type.88, () %tuple.60, (pred[64,2048]{1,0:T(8,128)(4,1)S(1)}, bf16[2,64,2,8,128]{4,3,2,1,0:T(8,128)(2,1)S(1)}, bf16[2048,2,128]{0,2,1:T(8,128)(2,1)}, ...), branch_computations={%region_14.15_spmd, %region_15.16_spmd} | conditional | flops 2705981440 | bytes 57466960 | solution.py:134
  169.5 2.5 fusion.48
  172.0 3.9 fusion.42
  175.9 2.8 multiply_convert_fusion
  178.7 2.1 fusion.45
  180.8 1.8 fusion.41
  182.6 15.8 %conditional.7 = (f32[2048,2,128]{2,0,1:T(8,128)S(1)}, f32[2048,2,128]{2,0,1:T(8,128)}, f32[1,2,8,64,128]{4,3,2,1,0:T(8,128)}) conditional(s32[]{:T(128)} %convert_element_type.96, (f32[2048,2,128]{2,0,1:T(8,128)S(1)}, f32[2048,2,128]{2,0,1:T(8,128)}) %tuple.62, (pred[64,2048]{1,0:T(8,128)(4,1)S(1)}, bf16[2,64,2,8,128]{4,3,2,1,0:T(8,128)(2,1)S(1)}, ...), branch_computations={%region_16.17_spmd, %region_17.18_spmd} | conditional | flops 2707030016 | bytes 61661264 | solution.py:134
  183.2 2.5 fusion.70
  185.7 5.2 fusion.63
  190.9 2.8 multiply_convert_fusion.1
  193.8 2.1 fusion.67
  195.8 2.5 fusion.66
  200.5 12.8 %copy.82 = bf16[2048,2,2,128]{3,2,1,0:T(2,128)(2,1)S(1)} copy(bf16[2048,2,2,128]{3,0,2,1:T(8,128)(2,1)S(1)} %pad_maximum_fusion) | data formatting | bytes 4194304 | tf_op jit(solution)/shard_map/stack | solution.py:139
  213.3 2.2 convert_element_type.102
  220.5 64.4 %reduce-scatter.2.cloned.1.call-done = bf16[128,512]{1,0:T(8,128)(2,1)} async-done(((bf16[2048,512]{1,0:T(8,128)(2,1)}), bf16[128,512]{1,0:T(8,128)(2,1)}) %reduce-scatter.2.cloned.1.call-update) | async-done | bytes 131088 | tf_op jit(solution)/shard_map/reduce_scatter | solution.py:142
  285.8 704.7 %all-reduce = (f32[2048]{0:T(1024)S(1)}, f32[256]{0:T(256)S(1)}) all-reduce(f32[2048]{0:T(1024)S(1)} %bitcast.250, f32[256]{0:T(256)S(1)} %convert_reduce_fusion), channel_id=1, replica_groups=mesh['dp'=16,'ctx'=16,'tp'=2] {'dp','ctx'}, use_global_device_ids=true, to_apply=%region_20.21 | all-reduce | flops 2304 | bytes 18432 | tf_op jit(solution)/shard_map/psum | solution.py:158
  (70 shorter events, 26.5 us)
Async XLA Ops:
  7.2 74.8 %all-gather.6.cloned.1.call-start = ((), (), s32[]{:S(2)}) async-start(), calls=%async_computation.3 | async-start | bytes 1114112 | tf_op jit(solution)/shard_map/all_gather | solution.py:51
  8.8 143.9 %all-gather.4.cloned.1.call-start = ((), (), s32[]{:S(2)}) async-start(), calls=%async_computation.1 | async-start | bytes 1114112 | tf_op jit(solution)/shard_map/all_gather | solution.py:52
  11.2 273.7 %reduce-scatter.2.cloned.1.call-start = ((), (), s32[]{:S(2)}) async-start(), calls=%async_computation.2 | async-start | bytes 2228224 | tf_op jit(solution)/shard_map/reduce_scatter | solution.py:142
  152.7 3.0 copy-start.3
  160.0 3.1 copy-start.4
  172.0 3.9 copy-start.5
  175.9 2.8 copy-start
  185.7 5.3 copy-start.6
  190.9 2.8 copy-start.1
  198.5 17.1 %copy-start.2 = (bf16[2,2,8,64,128]{4,2,1,3,0:T(8,128)(2,1)S(1)}, bf16[2,2,8,64,128]{4,2,1,3,0:T(8,128)(2,1)}, u32[]{:S(2)}) copy-start(bf16[2,2,8,64,128]{4,2,1,3,0:T(8,128)(2,1)} %get-tuple-element.195) | copy-start | bytes 1572868
Sparse Core Ops, SparseCore 0:
  10.6 71.3 all-gather.5
  84.6 68.1 all-gather.3
  215.7 69.1 reduce-scatter.1
where the time goes:
time: 1000 us
  blocking collectives  705 us (70%)
  waiting for transfers between devices  199 us (20%)
  matrix products  37.2 us (4%)
  local copies, waits for them, and re-layouts  24.6 us (2%)
  other arithmetic  18 us (2%)
  between operations  15.2 us (2%)
    psum x1, blocking collectives, shards(): totals = lax.psum((q_sum, v_sum), ('dp', 'ctx'))  705 us
    all_gather x1, waiting for transfers between devices, shards(): block_v = lax.all_gather(values, 'ctx', axis=0, tiled=True)  70.7 us
    reduce_scatter x1, waiting for transfers between devices, shards(): lax.psum_scatter(kv_acc.reshape(total_rows, 2 * kv_width).astype(jnp.bflo...  64.4 us
    all_gather x1, waiting for transfers between devices, shards(): block_k = lax.all_gather(keys, 'ctx', axis=0, tiled=True)  64.1 us
  transfers between devices with their start and end apart: 3, of which 3 were waited for; matrix products, arithmetic and copies ran while one was open for 1% of the time, Pallas kernels for 0%

commit v1 on v0

v1 whole, which is shorter than its diff:
```python
import math

import jax
import jax.numpy as jnp
from jax import lax
from jax.experimental import pallas as pl
from jax.experimental.pallas import tpu as pltpu
from jax.sharding import PartitionSpec as P

HEAD_DIM = 128
SCALE = HEAD_DIM ** -0.5
LOG2E = math.log2(math.e)
NEG = -1e30
BLOCK = 128
KV = 2
GROUP = 8
TILES = 4
RING = 16
CHUNKS = 7
F32 = jnp.float32
BF16 = jnp.bfloat16


def slot_left(k):
    return k + 1 + ((k + 11) // 16) * (k - 5)


def slot_right(k):
    return 17 - k + ((k + 12) // 16) * (3 * k - 18)


def nearest(c):
    far = (c + 13) // 16
    return (2 * c - 1) * (1 - far) + (c + 2) * far


def kernel(
    q_hbm, qb_ref, k_hbm, v_hbm, vb_ref, g_hbm, len_ref,
    attn_hbm, qg_hbm, kg_ref, vg_ref, qbg_ref, vbg_ref,
    q_in, k_in, v_in, g_in, q_rows, g_rows, q_cols, g_cols, kv, scores, top, total, delta, acc, q_acc, terms,
    attn_out, qg_out, v_sum,
    left_in, right_in, left_out, right_out, share, share_z, part, share_d, final,
    load_sem, store_sem, ag_send, ag_recv, rs_send, rs_recv, ar_send, ar_recv,
):
    dp, me, tp = lax.axis_index("dp"), lax.axis_index("ctx"), lax.axis_index("tp")
    dps = lax.axis_size("dp")
    right, left = lax.rem(me + 1, RING), lax.rem(me + RING - 1, RING)
    to_right, to_left = (dp, right, tp), (dp, left, tp)

    def z_peer(o):
        return lax.rem(me + o, RING)

    def d_peer(o):
        return lax.rem(dp + o, dps)

    loads = [
        pltpu.make_async_copy(src, dst, load_sem.at[i])
        for i, (src, dst) in enumerate(((k_hbm, k_in), (v_hbm, v_in), (q_hbm, q_in), (g_hbm, g_in)))
    ]
    for copy in loads:
        copy.start()

    barrier = pltpu.get_barrier_semaphore()

    def greet_z(o, _):
        pl.semaphore_signal(barrier, inc=1, device_id=(dp, z_peer(o), tp), device_id_type=pl.DeviceIdType.MESH)
        return 0

    def greet_d(o, _):
        pl.semaphore_signal(barrier, inc=1, device_id=(d_peer(o), me, tp), device_id_type=pl.DeviceIdType.MESH)
        return 0

    lax.fori_loop(1, RING, greet_z, 0)
    lax.fori_loop(1, dps, greet_d, 0)

    def remote(src, dst, send, recv, device):
        return pltpu.make_async_remote_copy(
            src_ref=src, dst_ref=dst, send_sem=send, recv_sem=recv, device_id=device, device_id_type=pl.DeviceIdType.MESH
        )

    def ag(way, src, dst, k, h):
        return remote(kv.at[src, h], kv.at[dst, h], ag_send.at[way, k, h], ag_recv.at[way, k, h], (to_right, to_left)[way])

    loads[0].wait()
    loads[1].wait()
    values = (v_in[...].astype(F32) + vb_ref[...].astype(F32)).astype(BF16)
    for h in range(KV):
        kv[0, h, 0] = k_in[:, h * 128:(h + 1) * 128]
        kv[0, h, 1] = values[:, h * 128:(h + 1) * 128]
    kv[1] = jnp.zeros((KV, 2, BLOCK, HEAD_DIM), BF16)
    pl.semaphore_wait(barrier, RING - 1 + dps - 1)
    for h in range(KV):
        ag(0, 0, slot_left(1), 1, h).start()
        ag(1, 0, slot_right(1), 1, h).start()

    loads[2].wait()
    loads[3].wait()
    for h in range(KV):
        for j in range(TILES):
            for e in range(2):
                at = (h * GROUP + j * 2 + e) * 128
                rows = slice(e * 128, (e + 1) * 128)
                block = (q_in[:, at:at + 128].astype(F32) + qb_ref[:, at:at + 128].astype(F32)).astype(BF16)
                q_rows[h, j, rows, :] = block
                q_cols[h, j, :, rows] = block.T
                block = g_in[:, at:at + 128]
                g_rows[h, j, rows, :] = block
                g_cols[h, j, :, rows] = block.T
    top[...] = jnp.full(top.shape, NEG, F32)
    total[...] = jnp.zeros(total.shape, F32)
    acc[...] = jnp.zeros(acc.shape, F32)
    q_acc[...] = jnp.zeros(q_acc.shape, F32)
    v_sum[...] = jnp.zeros(v_sum.shape, F32)
    share[...] = jnp.zeros(share.shape, F32)

    position = me * BLOCK + lax.broadcasted_iota(jnp.int32, (1, BLOCK), 1)
    begin = jnp.zeros((1, BLOCK), jnp.int32)
    end = jnp.int32(0)
    for d in range(len_ref.shape[1]):
        end = end + len_ref[0, d]
        begin = jnp.where(position >= end, end, begin)

    def forward(c, h):
        near = nearest(c)
        far = jnp.where(c == 0, -1, jnp.where(c <= 2, 2 * c, 15 - c))
        offset = lax.broadcasted_iota(jnp.int32, (BLOCK, BLOCK), 0)
        bias = []
        for d in (jnp.where(c == 0, 0, near), far):
            at = (me - d) * BLOCK + offset
            bias.append(jnp.where((at >= begin) & (at <= position), 0.0, NEG).astype(F32))
        bias = jnp.concatenate(bias, axis=0)
        bias = jnp.concatenate([bias, bias], axis=1)
        pair = kv[pl.ds(2 * c, 2), h]
        keys = pair[:, 0].reshape(2 * BLOCK, HEAD_DIM)
        values_t = pair[:, 1].reshape(2 * BLOCK, HEAD_DIM).T
        for j in range(TILES):
            score = jnp.dot(keys, q_cols[h, j], preferred_element_type=F32) * (SCALE * LOG2E) + bias
            scores[c, h, j] = score
            old = top[h, j]
            new = jnp.maximum(old, jnp.max(score, axis=0, keepdims=True))
            fade = jnp.exp2(old - new)
            weights = jnp.exp2(score - new)
            top[h, j] = new
            total[h, j] = total[h, j] * fade + jnp.sum(weights, axis=0, keepdims=True)
            acc[h, j] = acc[h, j] * fade + jnp.dot(values_t, weights.astype(BF16), preferred_element_type=F32)

    def pass_on(k, h):
        @pl.when((k < 8) | (h == 0))
        def _():
            here = slot_left(k)
            ag(0, here, here, k, h).wait_recv()

            @pl.when((k < 7) | ((k == 7) & (h == 0)))
            def _():
                ag(0, here, slot_left(k + 1), k + 1, h).start()

        @pl.when(k < 8)
        def _():
            here = slot_right(k)
            ag(1, here, here, k, h).wait_recv()

            @pl.when(k < 7)
            def _():
                ag(1, here, slot_right(k + 1), k + 1, h).start()

            @pl.when((k == 7) & (h == 1))
            def _():
                ag(1, here, 12, 8, h).start()

        @pl.when((k == 8) & (h == 1))
        def _():
            ag(1, 12, 12, 8, h).wait_recv()

    def forward_step(i, _):
        c, h = i // 2, i % 2

        @pl.when((c >= 1) & (c <= 2))
        def _():
            @pl.when(h == 0)
            def _():
                pass_on(2 * c - 1, 0)
                pass_on(2 * c - 1, 1)

            pass_on(2 * c, h)

        @pl.when(c >= 3)
        def _():
            pass_on(c + 2, h)

        live = me >= nearest(c)

        @pl.when(live)
        def _():
            forward(c, h)

        @pl.when(jnp.logical_not(live))
        def _():
            terms[pl.ds(2 * c, 2), h] = jnp.zeros((2, 2, BLOCK, HEAD_DIM), F32)

        return 0

    lax.fori_loop(0, CHUNKS * KV, forward_step, 0)

    for h in range(KV):
        for j in range(TILES):
            amount = total[h, j]
            out = (acc[h, j] * (1.0 / amount)).astype(BF16)
            delta[h, j] = jnp.sum(out.astype(F32) * g_cols[h, j].astype(F32), axis=0, keepdims=True)
            top[h, j] = top[h, j] + jnp.log2(amount)
            for e in range(2):
                at = (h * GROUP + j * 2 + e) * 128
                attn_out[:, at:at + 128] = out[:, e * 128:(e + 1) * 128].T
    store_attn = pltpu.make_async_copy(attn_out, attn_hbm, store_sem.at[0])
    store_attn.start()

    def backward(c, h):
        pair = kv[pl.ds(2 * c, 2), h]
        keys_t = pair[:, 0].reshape(2 * BLOCK, HEAD_DIM).T
        values = pair[:, 1].reshape(2 * BLOCK, HEAD_DIM)
        v_term = jnp.zeros((2 * BLOCK, HEAD_DIM), F32)
        k_term = jnp.zeros((2 * BLOCK, HEAD_DIM), F32)
        for j in range(TILES):
            probs = jnp.exp2(scores[c, h, j] - top[h, j])
            dprob = jnp.dot(values, g_cols[h, j], preferred_element_type=F32)
            dscore = (probs * (dprob - delta[h, j])).astype(BF16)
            v_term += jnp.dot(probs.astype(BF16), g_rows[h, j], preferred_element_type=F32)
            k_term += jnp.dot(dscore, q_rows[h, j], preferred_element_type=F32)
            q_acc[h, j] += jnp.dot(keys_t, dscore, preferred_element_type=F32)
        terms[pl.ds(2 * c, 2), h, 0] = (k_term * SCALE).reshape(2, BLOCK, HEAD_DIM)
        terms[pl.ds(2 * c, 2), h, 1] = v_term.reshape(2, BLOCK, HEAD_DIM)
        v_sum[h] += jnp.sum(v_term, axis=0, keepdims=True)

    def rs(way, src, k, h):
        return remote(src, (left_in, right_in)[way].at[k - 1, h], rs_send.at[way, k, h], rs_recv.at[way, k - 1, h], (to_left, to_right)[way])

    def arrived(way, k, h):
        into = (left_in, right_in)[way].at[k, h]
        remote(into, into, rs_send.at[way, k, h], rs_recv.at[way, k, h], (to_left, to_right)[way]).wait_recv()

    def begin_sum(way, k, h, slot):
        held = (left_out, right_out)[way]
        held[k, h] = terms[slot, h].astype(BF16)
        rs(way, held.at[k, h], k, h).start()

    def add_sum(way, k, h, slot):
        arrived(way, k, h)
        held = (left_out, right_out)[way]
        held[k, h] = (terms[slot, h] + (left_in, right_in)[way][k, h].astype(F32)).astype(BF16)
        rs(way, held.at[k, h], k, h).start()

    def backward_step(i, h):
        c = CHUNKS - 1 - i

        @pl.when(me >= nearest(c))
        def _():
            backward(c, h)

        k = 8 - i

        @pl.when(((i == 0) & (h == 0)) | ((i == 1) & (h == 1)))
        def _():
            begin_sum(0, k, h, slot_left(k))

        @pl.when((i >= 2) | ((i == 1) & (h == 0)))
        def _():
            add_sum(0, k, h, slot_left(k))

        k2 = 7 - i

        @pl.when((i == 0) & (h == 0))
        def _():
            begin_sum(1, k2, h, slot_right(k2))

        @pl.when((i == 0) & (h == 1))
        def _():
            begin_sum(1, 8, h, 12)

        @pl.when(((i >= 1) & (i <= 3)) | ((i == 0) & (h == 1)))
        def _():
            add_sum(1, k2, h, slot_right(k2))

        @pl.when((i >= 4) & (i <= 6))
        def _():
            arrived(1, k2, h)
            rs(1, right_in.at[k2, h], k2, h).start()

    def backward_loop(n, _):
        backward_step(n // 2, n % 2)
        return 0

    lax.fori_loop(0, CHUNKS * KV, backward_loop, 0)

    for h in range(KV):
        for j in range(TILES):
            for e in range(2):
                head = h * GROUP + j * 2 + e
                grad = q_acc[h, j, :, e * 128:(e + 1) * 128].T * SCALE
                share[head, 0:1, :] = jnp.sum(grad, axis=0, keepdims=True)
                qg_out[:, head * 128:(head + 1) * 128] = grad.astype(BF16)
        share[h, 1:2, :] = v_sum[h]
    store_qg = pltpu.make_async_copy(qg_out, qg_hbm, store_sem.at[1])
    store_qg.start()

    def ar_z(o):
        return remote(share.at[z_peer(o)], share_z.at[o], ar_send.at[0, o], ar_recv.at[0, o], (dp, z_peer(o), tp))

    def ar_d(o):
        return remote(part, share_d.at[o], ar_send.at[1, o], ar_recv.at[1, o], (d_peer(o), me, tp))

    def ar_back(o):
        return remote(final.at[me], final.at[me], ar_send.at[2, o], ar_recv.at[2, o], (dp, z_peer(o), tp))

    def ar_back_in(o):
        source = lax.rem(me + RING - o, RING)
        return remote(final.at[source], final.at[source], ar_send.at[2, o], ar_recv.at[2, o], (dp, z_peer(o), tp))

    def each(last, act):
        def body(o, _):
            act(o)
            return 0

        lax.fori_loop(1, last, body, 0)

    each(RING, lambda o: ar_z(o).start())
    for h in range(KV):
        add_sum(0, 1, h, slot_left(1))

    each(RING, lambda o: ar_z(o).wait_recv())
    share_z[0] = share[me]
    part[...] = jnp.sum(share_z[...], axis=0)
    each(dps, lambda o: ar_d(o).start())
    each(dps, lambda o: ar_d(o).wait_recv())
    share_d[0] = part[...]
    final[me] = jnp.sum(share_d[...], axis=0) * (1.0 / dps)
    each(RING, lambda o: ar_back(o).start())

    for h in range(KV):
        arrived(0, 0, h)
        arrived(1, 0, h)
        both = terms[0, h] + left_in[0, h].astype(F32) + right_in[0, h].astype(F32)
        kg_ref[:, h * 128:(h + 1) * 128] = both[0].astype(BF16)
        vg_ref[:, h * 128:(h + 1) * 128] = both[1].astype(BF16)

    each(RING, lambda o: ar_back_in(o).wait_recv())
    for p in range(RING):
        qbg_ref[p:p + 1, :] = final[p, 0:1, :]
    for h in range(KV):
        vbg_ref[h:h + 1, :] = final[h, 1:2, :]

    def sent(n, _):
        k, h = n // 2 + 1, n % 2
        ag(0, 0, 0, k, h).wait_send()
        ag(1, 0, 0, k, h).wait_send()
        rs(0, left_out.at[k, h], k, h).wait_send()
        rs(1, right_out.at[k, h], k, h).wait_send()
        return 0

    lax.fori_loop(0, 14, sent, 0)
    ag(0, 0, 0, 8, 0).wait_send()
    ag(1, 0, 0, 8, 1).wait_send()
    rs(0, left_out.at[8, 0], 8, 0).wait_send()
    rs(1, right_out.at[8, 1], 8, 1).wait_send()
    each(RING, lambda o: ar_z(o).wait_send())
    each(dps, lambda o: ar_d(o).wait_send())
    each(RING, lambda o: ar_back(o).wait_send())
    store_attn.wait()
    store_qg.wait()


def shards(q_proj, q_bias, k_proj, v_proj, v_bias, dout, lengths):
    width, kv_width = q_proj.shape[2], k_proj.shape[2]
    dps = lax.axis_size("dp")
    any_space = pl.BlockSpec(memory_space=pl.ANY)
    vmem = pl.BlockSpec(memory_space=pltpu.VMEM)
    block = (KV, 2, BLOCK, HEAD_DIM)
    attn, q_grad, k_grad, v_grad, q_sums, v_sums = pl.pallas_call(
        kernel,
        out_shape=(
            jax.ShapeDtypeStruct((BLOCK, width), BF16),
            jax.ShapeDtypeStruct((BLOCK, width), BF16),
            jax.ShapeDtypeStruct((BLOCK, kv_width), BF16),
            jax.ShapeDtypeStruct((BLOCK, kv_width), BF16),
            jax.ShapeDtypeStruct((KV * GROUP, HEAD_DIM), F32),
            jax.ShapeDtypeStruct((KV, HEAD_DIM), F32),
        ),
        in_specs=[any_space, vmem, any_space, any_space, vmem, any_space, pl.BlockSpec(memory_space=pltpu.SMEM)],
        out_specs=(any_space, any_space, vmem, vmem, vmem, vmem),
        scratch_shapes=[
            pltpu.VMEM((BLOCK, width), BF16),
            pltpu.VMEM((BLOCK, kv_width), BF16),
            pltpu.VMEM((BLOCK, kv_width), BF16),
            pltpu.VMEM((BLOCK, width), BF16),
            pltpu.VMEM((KV, TILES, 2 * BLOCK, HEAD_DIM), BF16),
            pltpu.VMEM((KV, TILES, 2 * BLOCK, HEAD_DIM), BF16),
            pltpu.VMEM((KV, TILES, HEAD_DIM, 2 * BLOCK), BF16),
            pltpu.VMEM((KV, TILES, HEAD_DIM, 2 * BLOCK), BF16),
            pltpu.VMEM((17,) + block, BF16),
            pltpu.VMEM((CHUNKS, KV, TILES, 2 * BLOCK, 2 * BLOCK), F32),
            pltpu.VMEM((KV, TILES, 1, 2 * BLOCK), F32),
            pltpu.VMEM((KV, TILES, 1, 2 * BLOCK), F32),
            pltpu.VMEM((KV, TILES, 1, 2 * BLOCK), F32),
            pltpu.VMEM((KV, TILES, HEAD_DIM, 2 * BLOCK), F32),
            pltpu.VMEM((KV, TILES, HEAD_DIM, 2 * BLOCK), F32),
            pltpu.VMEM((2 * CHUNKS,) + block, F32),
            pltpu.VMEM((BLOCK, width), BF16),
            pltpu.VMEM((BLOCK, width), BF16),
            pltpu.VMEM((KV, 1, HEAD_DIM), F32),
            pltpu.VMEM((8,) + block, BF16),
            pltpu.VMEM((8,) + block, BF16),
            pltpu.VMEM((9,) + block, BF16),
            pltpu.VMEM((9,) + block, BF16),
            pltpu.VMEM((RING, 8, HEAD_DIM), F32),
            pltpu.VMEM((RING, 8, HEAD_DIM), F32),
            pltpu.VMEM((8, HEAD_DIM), F32),
            pltpu.VMEM((dps, 8, HEAD_DIM), F32),
            pltpu.VMEM((RING, 8, HEAD_DIM), F32),
            pltpu.SemaphoreType.DMA((4,)),
            pltpu.SemaphoreType.DMA((2,)),
            pltpu.SemaphoreType.DMA((2, 9, KV)),
            pltpu.SemaphoreType.DMA((2, 9, KV)),
            pltpu.SemaphoreType.DMA((2, 9, KV)),
            pltpu.SemaphoreType.DMA((2, 9, KV)),
            pltpu.SemaphoreType.DMA((3, RING)),
            pltpu.SemaphoreType.DMA((3, RING)),
        ],
        compiler_params=pltpu.CompilerParams(
            collective_id=0, has_side_effects=True, vmem_limit_bytes=48 * 2**20
        ),
        cost_estimate=pl.CostEstimate(flops=6 * 10**9, bytes_accessed=3 * 10**6, transcendentals=7 * 10**6),
    )(
        q_proj[0],
        q_bias.reshape(1, -1),
        k_proj[0],
        v_proj[0],
        v_bias.reshape(1, -1),
        dout[0],
        lengths,
    )
    return attn[None], q_grad[None], k_grad[None], v_grad[None], q_sums.reshape(-1), v_sums.reshape(-1)


def solution(mesh):
    placed = (
        P("dp", "ctx", "tp"),
        P("tp"),
        P("dp", "ctx", "tp"),
        P("dp", "ctx", "tp"),
        P("tp"),
        P("dp", "ctx", "tp"),
        P("dp", None),
    )
    return jax.shard_map(
        shards,
        mesh=mesh,
        in_specs=placed,
        out_specs=(
            P("dp", "ctx", "tp"),
            P("dp", "ctx", "tp"),
            P("dp", "ctx", "tp"),
            P("dp", "ctx", "tp"),
            P("tp"),
            P("tp"),
        ),
        check_vma=False,
    )
```

time: 1000 us -> 113 us (0.11)
  the two profiles are of different devices: /device:TPU:0 before, /device:TPU:32 now
where the time goes in v1:
time: 113 us
  Pallas kernels  103 us (91%)
  local copies, waits for them, and re-layouts  9.09 us (8%)
    pallas_call x1, Pallas kernels, shards(): pl.pallas_call(kernel, out_shape=(jax.ShapeDtypeStruct((BLOCK, width), BF...  103 us
    unnamed x20, local copies, waits for them, and re-layouts  9.08 us

profile of v1, /device:TPU:32, one launch (start us, length us, event | category | flops | bytes accessed | tf_op | source)
XLA Modules:
  0.0 112.8 jit_solution(5681280372203984868)
XLA Ops:
  0.6 0.0 copy-start.5
  0.6 0.0 copy-start.6
  0.7 0.7 copy-done.6
  1.3 0.0 copy-done.5
  1.3 0.0 copy-start.4
  1.3 0.6 copy-done.4
  2.0 0.0 copy-start
  2.0 1.0 copy-done
  3.0 0.0 copy-start.1
  3.0 1.0 copy-done.1
  4.1 0.0 copy-start.2
  4.1 0.8 copy-done.2
  4.9 0.0 copy-start.3
  4.9 0.8 copy-done.3
  5.7 103.0 %shard_map.118 = (bf16[128,2048]{1,0:T(8,128)(2,1)S(1)}, bf16[128,2048]{1,0:T(8,128)(2,1)S(1)}, bf16[128,256]{1,0:T(8,128)(2,1)S(1)}, bf16[128,256]{1,0:T(8,128)...) custom-call(bf16[128,2048]{1,0:T(8,128)(2,1)S(1)} %bitcast.16, bf16[1,2048]{1,0:T(2,128)(2,1)S(1)} %reshape.24.qb_ref, ...), custom_call_target="tpu_custom_call" | custom-call | flops 6000000000 | bytes 3000000 | tf_op jit(solution)/shard_map/pallas_call | solution.py:376
  108.8 0.8 copy.19
  109.6 0.8 copy.20
  110.4 0.6 copy.21
  111.0 0.6 copy.22
  111.6 0.6 copy.23
  112.2 0.6 copy.24
  (2 shorter events, 0.0 us)
Async XLA Ops:
  0.6 0.7 copy-start.5
  0.6 0.7 copy-start.6
  1.3 0.7 copy-start.4
  2.0 1.0 copy-start
  3.0 1.0 copy-start.1
  4.1 0.8 copy-start.2
  4.9 0.8 copy-start.3

commit v2 on v1

v2 whole, which is shorter than its diff:
```python
import math

import jax
import jax.numpy as jnp
from jax import lax
from jax.experimental import pallas as pl
from jax.experimental.pallas import tpu as pltpu
from jax.sharding import PartitionSpec as P

HEAD_DIM = 128
SCALE = HEAD_DIM ** -0.5
LOG2E = math.log2(math.e)
NEG = -1e30
BLOCK = 128
KV = 2
GROUP = 8
TILES = 4
RING = 16
CHUNKS = 7
F32 = jnp.float32
BF16 = jnp.bfloat16

PAIRS = ((0, None), (3, 12), (1, 2), (4, 11), (5, 10), (6, 9), (7, 8))
SLOT = {d: 2 * c + n for c, pair in enumerate(PAIRS) for n, d in enumerate(pair) if d is not None}
NEXT = {1: 2, 3: 4, 4: 5, 5: 6, 6: 7, 12: 11, 11: 10, 10: 9, 9: 8}
FIRST = (12, 3, 1)
SUMS = {7: (6, -1), 6: (5, -1), 5: (4, -1), 4: (3, -1), 3: (2, -3), 2: (1, -1), 1: (0, -1),
        8: (9, 1), 9: (10, 1), 10: (11, 1), 11: (12, 1), 12: (7, 4)}
ROWS = 24


def nearest(c):
    return 3 * ((c + 6) // 7) - 2 * ((c + 5) // 7) + c * ((c + 4) // 7)


def kernel(
    q_hbm, qb_hbm, k_hbm, v_hbm, vb_hbm, g_hbm, len_hbm,
    attn_hbm, qg_hbm, kg_hbm, vg_hbm, qbg_hbm, vbg_hbm,
    attn_out, qg_out, kg_ref, vg_ref, qbg_ref, vbg_ref, q_in, qb_in, k_in, v_in, vb_in, g_in, lens, q_rows, g_rows, q_cols, g_cols, kv, scores, top, total, delta, acc, q_acc, terms,
    v_sum, sum_in, sum_out, share, share_d, part, share_z,
    load_sem, store_sem, ag_send, ag_recv, rs_send, rs_recv, ar_send, ar_recv,
):
    dp, me, tp = lax.axis_index("dp"), lax.axis_index("ctx"), lax.axis_index("tp")
    dps = lax.axis_size("dp")

    def z_peer(o):
        return lax.rem(me + RING + o, RING)

    def d_peer(o):
        return lax.rem(dp + o, dps)

    loads = [
        pltpu.make_async_copy(src, dst, load_sem.at[i])
        for i, (src, dst) in enumerate((
            (k_hbm, k_in), (v_hbm, v_in), (vb_hbm, vb_in), (q_hbm, q_in), (g_hbm, g_in), (qb_hbm, qb_in), (len_hbm, lens)))
    ]
    for copy in loads:
        copy.start()

    stores = [
        pltpu.make_async_copy(src, dst, store_sem.at[i])
        for i, (src, dst) in enumerate((
            (attn_out, attn_hbm), (qg_out, qg_hbm), (kg_ref, kg_hbm), (vg_ref, vg_hbm), (qbg_ref, qbg_hbm), (vbg_ref, vbg_hbm)))
    ]
    barrier = pltpu.get_barrier_semaphore()

    def greet_z(o, _):
        pl.semaphore_signal(barrier, inc=1, device_id=(dp, z_peer(o), tp), device_id_type=pl.DeviceIdType.MESH)
        return 0

    def greet_d(o, _):
        pl.semaphore_signal(barrier, inc=1, device_id=(d_peer(o), me, tp), device_id_type=pl.DeviceIdType.MESH)
        return 0

    lax.fori_loop(1, RING, greet_z, 0)
    lax.fori_loop(1, dps, greet_d, 0)

    def remote(src, dst, send, recv, device):
        return pltpu.make_async_remote_copy(
            src_ref=src, dst_ref=dst, send_sem=send, recv_sem=recv, device_id=device, device_id_type=pl.DeviceIdType.MESH
        )

    def held(d):
        return me >= d if d <= 7 else lax.rem(me + RING - d, RING) <= 7

    def ag(d, to, h, n):
        step = to - d if to <= 7 else (-4 if d == 0 else -1)
        return remote(kv.at[SLOT[d], h, n], kv.at[SLOT[to], h, n], ag_send.at[to, h, n], ag_recv.at[to, h, n], (dp, z_peer(step), tp))

    def sends(d, to):
        return (held(d) & (me + to - d < RING)) if to <= 7 else held(d)

    for copy in loads[:3]:
        copy.wait()
    for h in range(KV):
        cols = slice(h * 128, (h + 1) * 128)
        kv[0, h, 0] = k_in[:, cols]
        kv[0, h, 1] = (v_in[:, cols].astype(F32) + vb_in[h:h + 1, :].astype(F32)).astype(BF16)
    nothing = jnp.zeros((KV, 2, BLOCK, HEAD_DIM), BF16)
    kv[1] = nothing
    pl.semaphore_wait(barrier, RING - 1 + dps - 1)
    for to in FIRST:
        @pl.when(me <= 7 if to == 12 else me + to < RING)
        def _(to=to):
            for h in range(KV):
                for n in range(2):
                    ag(0, to, h, n).start()

    for d in (2, 8, 9, 10, 11, 12):
        @pl.when(jnp.logical_not(held(d)))
        def _(d=d):
            kv[SLOT[d]] = nothing

    for copy in loads[3:]:
        copy.wait()
    for h in range(KV):
        for j in range(TILES):
            for e in range(2):
                head = h * GROUP + j * 2 + e
                cols = slice(head * 128, (head + 1) * 128)
                rows = slice(e * 128, (e + 1) * 128)
                block = (q_in[:, cols].astype(F32) + qb_in[head:head + 1, :].astype(F32)).astype(BF16)
                q_rows[h, j, rows, :] = block
                q_cols[h, j, :, rows] = block.T
                block = g_in[:, cols]
                g_rows[h, j, rows, :] = block
                g_cols[h, j, :, rows] = block.T
    top[...] = jnp.full(top.shape, NEG, F32)
    total[...] = jnp.zeros(total.shape, F32)
    acc[...] = jnp.zeros(acc.shape, F32)
    q_acc[...] = jnp.zeros(q_acc.shape, F32)
    v_sum[...] = jnp.zeros(v_sum.shape, F32)
    share[...] = jnp.zeros(share.shape, F32)

    position = me * BLOCK + lax.broadcasted_iota(jnp.int32, (1, BLOCK), 1)
    begin = jnp.zeros((1, BLOCK), jnp.int32)
    end = jnp.int32(0)
    for d in range(lens.shape[1]):
        end = end + lens[0, d]
        begin = jnp.where(position >= end, end, begin)

    def forward(c, h):
        near = nearest(c)
        far = jnp.where(c == 0, -1, jnp.where(c == 1, 12, jnp.where(c == 2, 2, 14 - c)))
        offset = lax.broadcasted_iota(jnp.int32, (BLOCK, BLOCK), 0)
        bias = []
        for d in (near, far):
            at = (me - d) * BLOCK + offset
            bias.append(jnp.where((at >= begin) & (at <= position), 0.0, NEG).astype(F32))
        bias = jnp.concatenate(bias, axis=0)
        bias = jnp.concatenate([bias, bias], axis=1)
        pair = kv[pl.ds(2 * c, 2), h]
        keys = pair[:, 0].reshape(2 * BLOCK, HEAD_DIM)
        values_t = pair[:, 1].reshape(2 * BLOCK, HEAD_DIM).T
        for j in range(TILES):
            score = jnp.dot(keys, q_cols[h, j], preferred_element_type=F32) * (SCALE * LOG2E) + bias
            scores[c, h, j] = score
            old = top[h, j]
            new = jnp.maximum(old, jnp.max(score, axis=0, keepdims=True))
            fade = jnp.exp2(old - new)
            weights = jnp.exp2(score - new)
            top[h, j] = new
            total[h, j] = total[h, j] * fade + jnp.sum(weights, axis=0, keepdims=True)
            acc[h, j] = acc[h, j] * fade + jnp.dot(values_t, weights.astype(BF16), preferred_element_type=F32)

    def pass_on(d, h):
        @pl.when(held(d))
        def _():
            for n in range(2):
                ag(d, d, h, n).wait_recv()
                if d in NEXT:
                    to = NEXT[d]
                    if to <= 7:
                        @pl.when(me + 1 < RING)
                        def _():
                            ag(d, to, h, n).start()
                    else:
                        ag(d, to, h, n).start()

    arrivals = {
        2: [(d, h) for h in range(KV) for d in (1, 3, 12)],
        4: [(2, 0)],
        5: [(4, 0), (11, 0), (4, 1), (11, 1), (2, 1)],
        8: [(5, 0), (10, 0)],
        9: [(5, 1), (10, 1)],
        10: [(6, 0), (9, 0)],
        11: [(6, 1), (9, 1)],
        12: [(7, 0), (8, 0)],
        13: [(7, 1), (8, 1)],
    }

    def forward_step(u, _):
        for at, blocks in arrivals.items():
            @pl.when(u == at)
            def _(blocks=blocks):
                for d, h in blocks:
                    pass_on(d, h)

        c = u // 2

        @pl.when(me >= nearest(c))
        def _():
            forward(c, u % 2)

        return 0

    lax.fori_loop(0, CHUNKS * KV, forward_step, 0)

    for h in range(KV):
        for j in range(TILES):
            amount = total[h, j]
            out = (acc[h, j] * (1.0 / amount)).astype(BF16)
            delta[h, j] = jnp.sum(out.astype(F32) * g_cols[h, j].astype(F32), axis=0, keepdims=True)
            top[h, j] = top[h, j] + jnp.log2(amount)
            for e in range(2):
                at = (h * GROUP + j * 2 + e) * 128
                attn_out[:, at:at + 128] = out[:, e * 128:(e + 1) * 128].T

    stores[0].start()

    def backward(c, h):
        pair = kv[pl.ds(2 * c, 2), h]
        keys_t = pair[:, 0].reshape(2 * BLOCK, HEAD_DIM).T
        values = pair[:, 1].reshape(2 * BLOCK, HEAD_DIM)
        v_term = jnp.zeros((2 * BLOCK, HEAD_DIM), F32)
        k_term = jnp.zeros((2 * BLOCK, HEAD_DIM), F32)
        for j in range(TILES):
            probs = jnp.exp2(scores[c, h, j] - top[h, j])
            dprob = jnp.dot(values, g_cols[h, j], preferred_element_type=F32)
            dscore = (probs * (dprob - delta[h, j])).astype(BF16)
            v_term += jnp.dot(probs.astype(BF16), g_rows[h, j], preferred_element_type=F32)
            k_term += jnp.dot(dscore, q_rows[h, j], preferred_element_type=F32)
            q_acc[h, j] += jnp.dot(keys_t, dscore, preferred_element_type=F32)
        terms[pl.ds(2 * c, 2), h, 0] = (k_term * SCALE).reshape(2, BLOCK, HEAD_DIM)
        terms[pl.ds(2 * c, 2), h, 1] = v_term.reshape(2, BLOCK, HEAD_DIM)
        v_sum[h] += jnp.sum(v_term, axis=0, keepdims=True)

    def rs(d, h, n):
        to, step = SUMS[d]
        return remote(sum_out.at[d, h, n], sum_in.at[to, h, n], rs_send.at[d, h, n], rs_recv.at[to, h, n], (dp, z_peer(step), tp))

    def arrived(into, h, n):
        at = sum_in.at[into, h, n]
        remote(at, at, rs_send.at[into, h, n], rs_recv.at[into, h, n], (dp, z_peer(1), tp)).wait_recv()

    def send_sum(d, h):
        def send(mine, before):
            for n in range(2):
                amount = None
                if before:
                    arrived(d, h, n)
                    amount = sum_in[d, h, n]
                if mine:
                    term = terms[SLOT[d], h, n]
                    amount = (term if amount is None else term + amount.astype(F32)).astype(BF16)
                sum_out[d, h, n] = amount
                rs(d, h, n).start()

        if d in (7, 2, 8):
            pl.when(held(d))(lambda: send(True, False))
        elif d <= 7:
            pl.when((me >= d) & (me < RING - 1))(lambda: send(True, True))
            pl.when(me == RING - 1)(lambda: send(True, False))
        else:
            pl.when(me >= d)(lambda: send(True, True))
            pl.when(held(d) & (me < d))(lambda: send(False, True))

    leaving = {h: [(7, h), (8, h)] for h in range(KV)}
    for step, pair in enumerate(((6, 9), (5, 10), (4, 11), (3, 12)), 1):
        for h in range(KV):
            leaving[3 * step + h] = [(d, h) for d in pair]
    leaving[10].append((2, 0))
    leaving[11] = [(2, 1)]

    def backward_step(u, _):
        o = u // 2
        c = 6 - o - (o + 3) // 7 + 2 * ((o + 2) // 7) - (o + 1) // 7

        @pl.when(me >= nearest(c))
        def _():
            backward(c, u % 2)

        for at, sums in leaving.items():
            @pl.when(u == at)
            def _(sums=sums):
                for d, h in sums:
                    send_sum(d, h)

        return 0

    lax.fori_loop(0, CHUNKS * KV, backward_step, 0)

    for h in range(KV):
        for j in range(TILES):
            for e in range(2):
                head = h * GROUP + j * 2 + e
                grad = q_acc[h, j, :, e * 128:(e + 1) * 128].T * SCALE
                share[head:head + 1, :] = jnp.sum(grad, axis=0, keepdims=True)
                qg_out[:, head * 128:(head + 1) * 128] = grad.astype(BF16)
        share[KV * GROUP + h:KV * GROUP + h + 1, :] = v_sum[h]

    stores[1].start()

    def ar_d(o):
        return remote(share, share_d.at[o], ar_send.at[0, o], ar_recv.at[0, o], (d_peer(o), me, tp))

    def ar_z(o):
        return remote(part, share_z.at[o], ar_send.at[1, o], ar_recv.at[1, o], (dp, z_peer(o), tp))

    def each(last, act):
        def body(o, _):
            act(o)
            return 0

        lax.fori_loop(1, last, body, 0)

    def farthest_first(act):
        def body(i, _):
            act(RING // 2 + ((i + 1) // 2) * (1 - 2 * ((i + 1) % 2)))
            return 0

        lax.fori_loop(0, RING - 1, body, 0)

    each(dps, lambda o: ar_d(o).start())
    for h in range(KV):
        send_sum(1, h)
    each(dps, lambda o: ar_d(o).wait_recv())
    share_d[0] = share[...]
    part[...] = jnp.sum(share_d[...], axis=0)
    farthest_first(lambda o: ar_z(o).start())

    for h in range(KV):
        for d, into in ((1, 0), (3, 2), (12, 7)):
            @pl.when(me <= 7 if d == 12 else me + d < RING)
            def _(into=into, h=h):
                for n in range(2):
                    arrived(into, h, n)
                    terms[0, h, n] = terms[0, h, n] + sum_in[into, h, n].astype(F32)
        kg_ref[:, h * 128:(h + 1) * 128] = terms[0, h, 0].astype(BF16)
        vg_ref[:, h * 128:(h + 1) * 128] = terms[0, h, 1].astype(BF16)

    stores[2].start()
    stores[3].start()

    for to in FIRST:
        @pl.when(me <= 7 if to == 12 else me + to < RING)
        def _(to=to):
            for h in range(KV):
                for n in range(2):
                    ag(0, to, h, n).wait_send()
    for d, to in NEXT.items():
        @pl.when(sends(d, to))
        def _(d=d, to=to):
            for h in range(KV):
                for n in range(2):
                    ag(d, to, h, n).wait_send()
    for d in SUMS:
        @pl.when(held(d))
        def _(d=d):
            for h in range(KV):
                for n in range(2):
                    rs(d, h, n).wait_send()
    each(dps, lambda o: ar_d(o).wait_send())

    each(RING, lambda o: ar_z(o).wait_recv())
    share_z[0] = part[...]
    sums = jnp.sum(share_z[...], axis=0) * (1.0 / dps)
    qbg_ref[...] = sums[:KV * GROUP]
    vbg_ref[...] = sums[KV * GROUP:KV * GROUP + KV]
    stores[4].start()
    stores[5].start()
    each(RING, lambda o: ar_z(o).wait_send())
    for copy in stores:
        copy.wait()


def write_out(*refs):
    count = len(refs) // 2
    sem = refs[-1]
    copies = [pltpu.make_async_copy(refs[i], refs[count + i], sem.at[i]) for i in range(count)]
    for copy in copies:
        copy.start()
    for copy in copies:
        copy.wait()


def shards(q_proj, q_bias, k_proj, v_proj, v_bias, dout, lengths):
    width, kv_width = q_proj.shape[2], k_proj.shape[2]
    dps = lax.axis_size("dp")
    hbm = pl.BlockSpec(memory_space=pltpu.HBM)
    block = (KV, 2, BLOCK, HEAD_DIM)
    results = (
        jax.ShapeDtypeStruct((BLOCK, width), BF16),
        jax.ShapeDtypeStruct((BLOCK, width), BF16),
        jax.ShapeDtypeStruct((BLOCK, kv_width), BF16),
        jax.ShapeDtypeStruct((BLOCK, kv_width), BF16),
        jax.ShapeDtypeStruct((KV * GROUP, HEAD_DIM), F32),
        jax.ShapeDtypeStruct((KV, HEAD_DIM), F32),
    )
    held = pl.pallas_call(
        kernel,
        out_shape=results,
        in_specs=[hbm] * 7,
        out_specs=(hbm,) * 6,
        scratch_shapes=[
            *(pltpu.VMEM(result.shape, result.dtype) for result in results),
            pltpu.VMEM((BLOCK, width), BF16),
            pltpu.VMEM((KV * GROUP, HEAD_DIM), BF16),
            pltpu.VMEM((BLOCK, kv_width), BF16),
            pltpu.VMEM((BLOCK, kv_width), BF16),
            pltpu.VMEM((KV, HEAD_DIM), BF16),
            pltpu.VMEM((BLOCK, width), BF16),
            pltpu.SMEM(lengths.shape, jnp.int32),
            pltpu.VMEM((KV, TILES, 2 * BLOCK, HEAD_DIM), BF16),
            pltpu.VMEM((KV, TILES, 2 * BLOCK, HEAD_DIM), BF16),
            pltpu.VMEM((KV, TILES, HEAD_DIM, 2 * BLOCK), BF16),
            pltpu.VMEM((KV, TILES, HEAD_DIM, 2 * BLOCK), BF16),
            pltpu.VMEM((2 * CHUNKS,) + block, BF16),
            pltpu.VMEM((CHUNKS, KV, TILES, 2 * BLOCK, 2 * BLOCK), F32),
            pltpu.VMEM((KV, TILES, 1, 2 * BLOCK), F32),
            pltpu.VMEM((KV, TILES, 1, 2 * BLOCK), F32),
            pltpu.VMEM((KV, TILES, 1, 2 * BLOCK), F32),
            pltpu.VMEM((KV, TILES, HEAD_DIM, 2 * BLOCK), F32),
            pltpu.VMEM((KV, TILES, HEAD_DIM, 2 * BLOCK), F32),
            pltpu.VMEM((2 * CHUNKS,) + block, F32),
            pltpu.VMEM((KV, 1, HEAD_DIM), F32),
            pltpu.VMEM((13,) + block, BF16),
            pltpu.VMEM((13,) + block, BF16),
            pltpu.VMEM((ROWS, HEAD_DIM), F32),
            pltpu.VMEM((dps, ROWS, HEAD_DIM), F32),
            pltpu.VMEM((ROWS, HEAD_DIM), F32),
            pltpu.VMEM((RING, ROWS, HEAD_DIM), F32),
            pltpu.SemaphoreType.DMA((7,)),
            pltpu.SemaphoreType.DMA((6,)),
            pltpu.SemaphoreType.DMA((13, KV, 2)),
            pltpu.SemaphoreType.DMA((13, KV, 2)),
            pltpu.SemaphoreType.DMA((13, KV, 2)),
            pltpu.SemaphoreType.DMA((13, KV, 2)),
            pltpu.SemaphoreType.DMA((2, RING)),
            pltpu.SemaphoreType.DMA((2, RING)),
        ],
        compiler_params=pltpu.CompilerParams(
            collective_id=0, has_side_effects=True, vmem_limit_bytes=60 * 2**20
        ),
        cost_estimate=pl.CostEstimate(flops=6 * 10**9, bytes_accessed=3 * 10**6, transcendentals=7 * 10**6),
        name="attention",
    )(
        q_proj[0],
        q_bias.reshape(-1, HEAD_DIM),
        k_proj[0],
        v_proj[0],
        v_bias.reshape(-1, HEAD_DIM),
        dout[0],
        lengths,
    )
    attn, q_grad, k_grad, v_grad, q_sums, v_sums = pl.pallas_call(
        write_out,
        out_shape=results,
        in_specs=[hbm] * 6,
        out_specs=(hbm,) * 6,
        scratch_shapes=[pltpu.SemaphoreType.DMA((6,))],
        compiler_params=pltpu.CompilerParams(vmem_limit_bytes=60 * 2**20),
        name="write_out",
    )(*held)
    return attn[None], q_grad[None], k_grad[None], v_grad[None], q_sums.reshape(-1), v_sums.reshape(-1)


def solution(mesh):
    placed = (
        P("dp", "ctx", "tp"),
        P("tp"),
        P("dp", "ctx", "tp"),
        P("dp", "ctx", "tp"),
        P("tp"),
        P("dp", "ctx", "tp"),
        P("dp", None),
    )
    return jax.shard_map(
        shards,
        mesh=mesh,
        in_specs=placed,
        out_specs=(
            P("dp", "ctx", "tp"),
            P("dp", "ctx", "tp"),
            P("dp", "ctx", "tp"),
            P("dp", "ctx", "tp"),
            P("tp"),
            P("tp"),
        ),
        check_vma=False,
    )
```

time: 113 us -> 128 us (1.13)
  Pallas kernels: 103 us -> 127 us
  local copies, waits for them, and re-layouts: 9.09 us -> 0 us
    pallas_call x1 -> x2, Pallas kernels: 103 us -> 127 us  [the longest x1 89.8 us: shards(): pl.pallas_call(kernel, out_shape=results, in_specs=[hbm] * 7, out_specs=(...]
    unnamed x20 -> x0, local copies, waits for them, and re-layouts: 9.08 us -> none
where the time goes in v2:
time: 128 us
  Pallas kernels  127 us (99%)
    pallas_call x1, Pallas kernels, shards(): pl.pallas_call(kernel, out_shape=results, in_specs=[hbm] * 7, out_specs=(...  89.8 us
    pallas_call x1, Pallas kernels, shards(): pl.pallas_call(write_out, out_shape=results, in_specs=[hbm] * 6, out_spec...  37.2 us

profile of v2, /device:TPU:32, one launch (start us, length us, event | category | flops | bytes accessed | tf_op | source)
XLA Modules:
  0.0 127.7 jit_solution(5190398187384093115)
XLA Ops:
  0.6 89.8 %attention.1 = (bf16[128,2048]{1,0:T(8,128)(2,1)}, bf16[128,2048]{1,0:T(8,128)(2,1)}, bf16[128,256]{1,0:T(8,128)(2,1)}, bf16[128,256]{1,0:T(8,128)(2,1)}, f32[16,128]{1,0:T(8,128)}, /*index=5*/f32[2,128]{1,0:T(2,128)}) custom-call(bf16[128,2048]{1,0:T(8,128)(2,1)} %bitcast.12, bf16[16,128]{1,0:T(8,128)(2,1)} %bitcast.21, bf16[128,256]{1,0:T(8,128)(2,1)} %bitcast.16, ...), custom_call_target="tpu_custom_call" | custom-call | flops 6000000000 | bytes 3000000 | tf_op jit(solution)/shard_map/attention/pallas_call | solution.py:400
  90.5 37.2 %write_out.1 = (bf16[128,2048]{1,0:T(8,128)(2,1)}, bf16[128,2048]{1,0:T(8,128)(2,1)}, bf16[128,256]{1,0:T(8,128)(2,1)}, bf16[128,256]{1,0:T(8,128)(2,1)}, f32[16,128]{1,0:T(8,128)}, /*index=5*/f32[2,128]{1,0:T(2,128)}) custom-call(bf16[128,2048]{1,0:T(8,128)(2,1)} %get-tuple-element.18.refs_0_, bf16[128,2048]{1,0:T(8,128)(2,1)} %get-tuple-element.19.refs_1_, ...), custom_call_target="tpu_custom_call" | custom-call | tf_op jit(solution)/shard_map/write_out/pallas_call | solution.py:456

commit v3 on v2

--- a/solution.py
+++ b/solution.py
@@ -26,6 +26,7 @@
 FIRST = (12, 3, 1)
 SUMS = {7: (6, -1), 6: (5, -1), 5: (4, -1), 4: (3, -1), 3: (2, -3), 2: (1, -1), 1: (0, -1),
         8: (9, 1), 9: (10, 1), 10: (11, 1), 11: (12, 1), 12: (7, 4)}
+STEPS = (1, -1, 3, -3, 4, -4)
 ROWS = 24
 
 
@@ -36,7 +37,7 @@
 def kernel(
     q_hbm, qb_hbm, k_hbm, v_hbm, vb_hbm, g_hbm, len_hbm,
     attn_hbm, qg_hbm, kg_hbm, vg_hbm, qbg_hbm, vbg_hbm,
-    attn_out, qg_out, kg_ref, vg_ref, qbg_ref, vbg_ref, q_in, qb_in, k_in, v_in, vb_in, g_in, lens, q_rows, g_rows, q_cols, g_cols, kv, scores, top, total, delta, acc, q_acc, terms,
+    attn_out, qg_out, kg_ref, vg_ref, qbg_ref, vbg_ref, q_in, qb_in, k_in, v_in, vb_in, g_in, lens, q_rows, g_rows, q_cols, g_cols, kv, scores, top, total, delta, acc, q_acc, terms, attn_t, probs_b, dscores,
     v_sum, sum_in, sum_out, share, share_d, part, share_z,
     load_sem, store_sem, ag_send, ag_recv, rs_send, rs_recv, ar_send, ar_recv,
 ):
@@ -64,15 +65,13 @@
     ]
     barrier = pltpu.get_barrier_semaphore()
 
-    def greet_z(o, _):
-        pl.semaphore_signal(barrier, inc=1, device_id=(dp, z_peer(o), tp), device_id_type=pl.DeviceIdType.MESH)
-        return 0
+    for step in STEPS:
+        pl.semaphore_signal(barrier, inc=1, device_id=(dp, z_peer(step), tp), device_id_type=pl.DeviceIdType.MESH)
 
     def greet_d(o, _):
         pl.semaphore_signal(barrier, inc=1, device_id=(d_peer(o), me, tp), device_id_type=pl.DeviceIdType.MESH)
         return 0
 
-    lax.fori_loop(1, RING, greet_z, 0)
     lax.fori_loop(1, dps, greet_d, 0)
 
     def remote(src, dst, send, recv, device):
@@ -98,7 +97,7 @@
         kv[0, h, 1] = (v_in[:, cols].astype(F32) + vb_in[h:h + 1, :].astype(F32)).astype(BF16)
     nothing = jnp.zeros((KV, 2, BLOCK, HEAD_DIM), BF16)
     kv[1] = nothing
-    pl.semaphore_wait(barrier, RING - 1 + dps - 1)
+    pl.semaphore_wait(barrier, len(STEPS) + dps - 1)
     for to in FIRST:
         @pl.when(me <= 7 if to == 12 else me + to < RING)
         def _(to=to):
@@ -148,20 +147,22 @@
             at = (me - d) * BLOCK + offset
             bias.append(jnp.where((at >= begin) & (at <= position), 0.0, NEG).astype(F32))
         bias = jnp.concatenate(bias, axis=0)
-        bias = jnp.concatenate([bias, bias], axis=1)
         pair = kv[pl.ds(2 * c, 2), h]
         keys = pair[:, 0].reshape(2 * BLOCK, HEAD_DIM)
         values_t = pair[:, 1].reshape(2 * BLOCK, HEAD_DIM).T
         for j in range(TILES):
-            score = jnp.dot(keys, q_cols[h, j], preferred_element_type=F32) * (SCALE * LOG2E) + bias
-            scores[c, h, j] = score
-            old = top[h, j]
-            new = jnp.maximum(old, jnp.max(score, axis=0, keepdims=True))
-            fade = jnp.exp2(old - new)
-            weights = jnp.exp2(score - new)
-            top[h, j] = new
-            total[h, j] = total[h, j] * fade + jnp.sum(weights, axis=0, keepdims=True)
-            acc[h, j] = acc[h, j] * fade + jnp.dot(values_t, weights.astype(BF16), preferred_element_type=F32)
+            for e in range(2):
+                at = slice(e * 128, (e + 1) * 128)
+                score = jnp.dot(keys, q_cols[h, j, :, at], preferred_element_type=F32) * (SCALE * LOG2E) + bias
+                scores[c, h, j, :, at] = score
+                old = top[h, j, :, at]
+                new = jnp.maximum(old, jnp.max(score, axis=0, keepdims=True))
+                fade = jnp.exp2(old - new)
+                weights = jnp.exp2(score - new)
+                top[h, j, :, at] = new
+                total[h, j, :, at] = total[h, j, :, at] * fade + jnp.sum(weights, axis=0, keepdims=True)
+                acc[h, j, :, at] = acc[h, j, :, at] * fade + jnp.dot(
+                    values_t, weights.astype(BF16), preferred_element_type=F32)
 
     def pass_on(d, h):
         @pl.when(held(d))
@@ -181,10 +182,8 @@
         2: [(d, h) for h in range(KV) for d in (1, 3, 12)],
         4: [(2, 0)],
         5: [(4, 0), (11, 0), (4, 1), (11, 1), (2, 1)],
-        8: [(5, 0), (10, 0)],
-        9: [(5, 1), (10, 1)],
-        10: [(6, 0), (9, 0)],
-        11: [(6, 1), (9, 1)],
+        8: [(5, 0), (10, 0), (5, 1), (10, 1)],
+        10: [(6, 0), (9, 0), (6, 1), (9, 1)],
         12: [(7, 0), (8, 0)],
         13: [(7, 1), (8, 1)],
     }
@@ -212,25 +211,31 @@
             out = (acc[h, j] * (1.0 / amount)).astype(BF16)
             delta[h, j] = jnp.sum(out.astype(F32) * g_cols[h, j].astype(F32), axis=0, keepdims=True)
             top[h, j] = top[h, j] + jnp.log2(amount)
-            for e in range(2):
-                at = (h * GROUP + j * 2 + e) * 128
-                attn_out[:, at:at + 128] = out[:, e * 128:(e + 1) * 128].T
-
-    stores[0].start()
+            attn_t[h, j] = out
+
+    def write_attention():
+        for h in range(KV):
+            for j in range(TILES):
+                for e in range(2):
+                    at = (h * GROUP + j * 2 + e) * 128
+                    attn_out[:, at:at + 128] = attn_t[h, j, :, e * 128:(e + 1) * 128].T
+        stores[0].start()
 
     def backward(c, h):
         pair = kv[pl.ds(2 * c, 2), h]
         keys_t = pair[:, 0].reshape(2 * BLOCK, HEAD_DIM).T
         values = pair[:, 1].reshape(2 * BLOCK, HEAD_DIM)
-        v_term = jnp.zeros((2 * BLOCK, HEAD_DIM), F32)
-        k_term = jnp.zeros((2 * BLOCK, HEAD_DIM), F32)
         for j in range(TILES):
+            at = slice(j * 256, (j + 1) * 256)
             probs = jnp.exp2(scores[c, h, j] - top[h, j])
             dprob = jnp.dot(values, g_cols[h, j], preferred_element_type=F32)
-            dscore = (probs * (dprob - delta[h, j])).astype(BF16)
-            v_term += jnp.dot(probs.astype(BF16), g_rows[h, j], preferred_element_type=F32)
-            k_term += jnp.dot(dscore, q_rows[h, j], preferred_element_type=F32)
-            q_acc[h, j] += jnp.dot(keys_t, dscore, preferred_element_type=F32)
+            dscores[:, at] = (probs * (dprob - delta[h, j])).astype(BF16)
+            probs_b[:, at] = probs.astype(BF16)
+        v_term = jnp.dot(probs_b[...], g_rows[h].reshape(GROUP * BLOCK, HEAD_DIM), preferred_element_type=F32)
+        k_term = jnp.dot(dscores[...], q_rows[h].reshape(GROUP * BLOCK, HEAD_DIM), preferred_element_type=F32)
+        q_term = jnp.dot(keys_t, dscores[...], preferred_element_type=F32)
+        for j in range(TILES):
+            q_acc[h, j] += q_term[:, j * 256:(j + 1) * 256]
         terms[pl.ds(2 * c, 2), h, 0] = (k_term * SCALE).reshape(2, BLOCK, HEAD_DIM)
         terms[pl.ds(2 * c, 2), h, 1] = v_term.reshape(2, BLOCK, HEAD_DIM)
         v_sum[h] += jnp.sum(v_term, axis=0, keepdims=True)
@@ -265,12 +270,15 @@
             pl.when(me >= d)(lambda: send(True, True))
             pl.when(held(d) & (me < d))(lambda: send(False, True))
 
-    leaving = {h: [(7, h), (8, h)] for h in range(KV)}
-    for step, pair in enumerate(((6, 9), (5, 10), (4, 11), (3, 12)), 1):
-        for h in range(KV):
-            leaving[3 * step + h] = [(d, h) for d in pair]
-    leaving[10].append((2, 0))
-    leaving[11] = [(2, 1)]
+    leaving = {
+        0: [(7, 0), (8, 0)],
+        1: [(7, 1), (8, 1)],
+        6: [(6, 0), (9, 0)],
+        7: [(6, 1), (9, 1)],
+        11: [(2, 0), (2, 1)],
+        12: [(5, 0), (10, 0)],
+        13: [(5, 1), (10, 1)],
+    }
 
     def backward_step(u, _):
         o = u // 2
@@ -279,6 +287,8 @@
         @pl.when(me >= nearest(c))
         def _():
             backward(c, u % 2)
+
+        pl.when(u == 2)(write_attention)
 
         for at, sums in leaving.items():
             @pl.when(u == at)
@@ -323,11 +333,17 @@
 
     each(dps, lambda o: ar_d(o).start())
     for h in range(KV):
-        send_sum(1, h)
+        send_sum(4, h)
+        send_sum(11, h)
     each(dps, lambda o: ar_d(o).wait_recv())
     share_d[0] = share[...]
     part[...] = jnp.sum(share_d[...], axis=0)
     farthest_first(lambda o: ar_z(o).start())
+    for h in range(KV):
+        send_sum(3, h)
+        send_sum(12, h)
+    for h in range(KV):
+        send_sum(1, h)
 
     for h in range(KV):
         for d, into in ((1, 0), (3, 2), (12, 7)):
@@ -375,12 +391,22 @@
 
 
 def write_out(*refs):
-    count = len(refs) // 2
-    sem = refs[-1]
-    copies = [pltpu.make_async_copy(refs[i], refs[count + i], sem.at[i]) for i in range(count)]
-    for copy in copies:
+    count = 6
+    sources, results, held = refs[:count], refs[count:2 * count], refs[2 * count:3 * count]
+    sem_in, sem_out = refs[3 * count:]
+    parts = []
+    for i in range(count):
+        rows = sources[i].shape[0]
+        step = 32 if rows == BLOCK else rows
+        parts += [(i, pl.ds(at, step)) for at in range(0, rows, step)]
+    ins = [pltpu.make_async_copy(sources[i].at[at], held[i].at[at], sem_in.at[n]) for n, (i, at) in enumerate(parts)]
+    outs = [pltpu.make_async_copy(held[i].at[at], results[i].at[at], sem_out.at[n]) for n, (i, at) in enumerate(parts)]
+    for copy in ins:
         copy.start()
-    for copy in copies:
+    for copy, onward in zip(ins, outs):
+        copy.wait()
+        onward.start()
+    for copy in outs:
         copy.wait()
 
 
@@ -423,6 +449,9 @@
             pltpu.VMEM((KV, TILES, HEAD_DIM, 2 * BLOCK), F32),
             pltpu.VMEM((KV, TILES, HEAD_DIM, 2 * BLOCK), F32),
             pltpu.VMEM((2 * CHUNKS,) + block, F32),
+            pltpu.VMEM((KV, TILES, HEAD_DIM, 2 * BLOCK), BF16),
+            pltpu.VMEM((2 * BLOCK, GROUP * BLOCK), BF16),
+            pltpu.VMEM((2 * BLOCK, GROUP * BLOCK), BF16),
             pltpu.VMEM((KV, 1, HEAD_DIM), F32),
             pltpu.VMEM((13,) + block, BF16),
             pltpu.VMEM((13,) + block, BF16),
@@ -458,7 +487,11 @@
         out_shape=results,
         in_specs=[hbm] * 6,
         out_specs=(hbm,) * 6,
-        scratch_shapes=[pltpu.SemaphoreType.DMA((6,))],
+        scratch_shapes=[
+            *(pltpu.VMEM(result.shape, result.dtype) for result in results),
+            pltpu.SemaphoreType.DMA((18,)),
+            pltpu.SemaphoreType.DMA((18,)),
+        ],
         compiler_params=pltpu.CompilerParams(vmem_limit_bytes=60 * 2**20),
         name="write_out",
     )(*held)

time: 128 us -> 88.6 us (0.69)
  the two profiles are of different devices: /device:TPU:32 before, /device:TPU:64 now
where the time goes in v3:
time: 88.6 us; the launch traced here: 88.4 us
  Pallas kernels  87.8 us (99%)
    pallas_call x1, Pallas kernels, shards(): pl.pallas_call(kernel, out_shape=results, in_specs=[hbm] * 7, out_specs=(...  85.5 us
    pallas_call x1, Pallas kernels, shards(): pl.pallas_call(write_out, out_shape=results, in_specs=[hbm] * 6, out_spec...  2.3 us

profile of v3, /device:TPU:64, one launch (start us, length us, event | category | flops | bytes accessed | tf_op | source)
XLA Modules:
  0.0 88.4 jit_solution(12023976754206588040)
XLA Ops:
  0.6 85.5 %attention.1 = (bf16[128,2048]{1,0:T(8,128)(2,1)}, bf16[128,2048]{1,0:T(8,128)(2,1)}, bf16[128,256]{1,0:T(8,128)(2,1)}, bf16[128,256]{1,0:T(8,128)(2,1)}, f32[16,128]{1,0:T(8,128)}, /*index=5*/f32[2,128]{1,0:T(2,128)}) custom-call(bf16[128,2048]{1,0:T(8,128)(2,1)} %bitcast.12, bf16[16,128]{1,0:T(8,128)(2,1)} %bitcast.21, bf16[128,256]{1,0:T(8,128)(2,1)} %bitcast.16, ...), custom_call_target="tpu_custom_call" | custom-call | flops 6000000000 | bytes 3000000 | tf_op jit(solution)/shard_map/attention/pallas_call | solution.py:426
  86.1 2.3 %write_out.1 = (bf16[128,2048]{1,0:T(8,128)(2,1)}, bf16[128,2048]{1,0:T(8,128)(2,1)}, bf16[128,256]{1,0:T(8,128)(2,1)}, bf16[128,256]{1,0:T(8,128)(2,1)}, f32[16,128]{1,0:T(8,128)}, /*index=5*/f32[2,128]{1,0:T(2,128)}) custom-call(bf16[128,2048]{1,0:T(8,128)(2,1)} %get-tuple-element.18.refs_0_, bf16[128,2048]{1,0:T(8,128)(2,1)} %get-tuple-element.19.refs_1_, ...), custom_call_target="tpu_custom_call" | custom-call | tf_op jit(solution)/shard_map/write_out/pallas_call | solution.py:485

commit v4 on v3

--- a/solution.py
+++ b/solution.py
@@ -20,25 +20,26 @@
 F32 = jnp.float32
 BF16 = jnp.bfloat16
 
-PAIRS = ((0, None), (3, 12), (1, 2), (4, 11), (5, 10), (6, 9), (7, 8))
+PAIRS = ((0, None), (3, 12), (4, 11), (1, 2), (5, 10), (6, 9), (7, 8))
 SLOT = {d: 2 * c + n for c, pair in enumerate(PAIRS) for n, d in enumerate(pair) if d is not None}
 NEXT = {1: 2, 3: 4, 4: 5, 5: 6, 6: 7, 12: 11, 11: 10, 10: 9, 9: 8}
 FIRST = (12, 3, 1)
+UNITS = 2 * CHUNKS * KV
 SUMS = {7: (6, -1), 6: (5, -1), 5: (4, -1), 4: (3, -1), 3: (2, -3), 2: (1, -1), 1: (0, -1),
         8: (9, 1), 9: (10, 1), 10: (11, 1), 11: (12, 1), 12: (7, 4)}
 STEPS = (1, -1, 3, -3, 4, -4)
-ROWS = 24
+ROWS = 2 * KV * GROUP
 
 
 def nearest(c):
-    return 3 * ((c + 6) // 7) - 2 * ((c + 5) // 7) + c * ((c + 4) // 7)
+    return (c + 2) * ((c + 6) // 7) - 4 * ((c + 4) // 7) + 3 * ((c + 3) // 7)
 
 
 def kernel(
     q_hbm, qb_hbm, k_hbm, v_hbm, vb_hbm, g_hbm, len_hbm,
     attn_hbm, qg_hbm, kg_hbm, vg_hbm, qbg_hbm, vbg_hbm,
     attn_out, qg_out, kg_ref, vg_ref, qbg_ref, vbg_ref, q_in, qb_in, k_in, v_in, vb_in, g_in, lens, q_rows, g_rows, q_cols, g_cols, kv, scores, top, total, delta, acc, q_acc, terms, attn_t, probs_b, dscores,
-    v_sum, sum_in, sum_out, share, share_d, part, share_z,
+    v_sum, sum_in, sum_out, share, share_d, part, share_z, sums,
     load_sem, store_sem, ag_send, ag_recv, rs_send, rs_recv, ar_send, ar_recv,
 ):
     dp, me, tp = lax.axis_index("dp"), lax.axis_index("ctx"), lax.axis_index("tp")
@@ -98,12 +99,16 @@
     nothing = jnp.zeros((KV, 2, BLOCK, HEAD_DIM), BF16)
     kv[1] = nothing
     pl.semaphore_wait(barrier, len(STEPS) + dps - 1)
-    for to in FIRST:
+
+    def send_own(to, h):
         @pl.when(me <= 7 if to == 12 else me + to < RING)
-        def _(to=to):
-            for h in range(KV):
-                for n in range(2):
-                    ag(0, to, h, n).start()
+        def _():
+            for n in range(2):
+                ag(0, to, h, n).start()
+
+    for h in range(KV):
+        send_own(12, h)
+        send_own(3, h)
 
     for d in (2, 8, 9, 10, 11, 12):
         @pl.when(jnp.logical_not(held(d)))
@@ -140,7 +145,7 @@
 
     def forward(c, h):
         near = nearest(c)
-        far = jnp.where(c == 0, -1, jnp.where(c == 1, 12, jnp.where(c == 2, 2, 14 - c)))
+        far = jnp.where(c == 0, -1, jnp.where(c == 3, 2, jnp.where(c <= 2, 13 - c, 14 - c)))
         offset = lax.broadcasted_iota(jnp.int32, (BLOCK, BLOCK), 0)
         bias = []
         for d in (near, far):
@@ -178,34 +183,7 @@
                     else:
                         ag(d, to, h, n).start()
 
-    arrivals = {
-        2: [(d, h) for h in range(KV) for d in (1, 3, 12)],
-        4: [(2, 0)],
-        5: [(4, 0), (11, 0), (4, 1), (11, 1), (2, 1)],
-        8: [(5, 0), (10, 0), (5, 1), (10, 1)],
-        10: [(6, 0), (9, 0), (6, 1), (9, 1)],
-        12: [(7, 0), (8, 0)],
-        13: [(7, 1), (8, 1)],
-    }
-
-    def forward_step(u, _):
-        for at, blocks in arrivals.items():
-            @pl.when(u == at)
-            def _(blocks=blocks):
-                for d, h in blocks:
-                    pass_on(d, h)
-
-        c = u // 2
-
-        @pl.when(me >= nearest(c))
-        def _():
-            forward(c, u % 2)
-
-        return 0
-
-    lax.fori_loop(0, CHUNKS * KV, forward_step, 0)
-
-    for h in range(KV):
+    def finish(h):
         for j in range(TILES):
             amount = total[h, j]
             out = (acc[h, j] * (1.0 / amount)).astype(BF16)
@@ -270,52 +248,95 @@
             pl.when(me >= d)(lambda: send(True, True))
             pl.when(held(d) & (me < d))(lambda: send(False, True))
 
+    arrivals = {
+        2: [(d, h) for h in range(KV) for d in (3, 12)],
+        4: [(1, 0), (1, 1), (4, 0), (11, 0), (4, 1), (11, 1)],
+        6: [(2, 0), (2, 1)],
+        8: [(5, 0), (10, 0), (5, 1), (10, 1)],
+        10: [(6, 0), (9, 0), (6, 1), (9, 1)],
+        12: [(7, 0), (8, 0)],
+        14: [(7, 1), (8, 1)],
+    }
     leaving = {
-        0: [(7, 0), (8, 0)],
-        1: [(7, 1), (8, 1)],
-        6: [(6, 0), (9, 0)],
-        7: [(6, 1), (9, 1)],
-        11: [(2, 0), (2, 1)],
-        12: [(5, 0), (10, 0)],
-        13: [(5, 1), (10, 1)],
+        13: [(7, 0), (8, 0)],
+        15: [(7, 1), (8, 1)],
+        17: [(6, 0), (9, 0)],
+        20: [(6, 1), (9, 1)],
+        23: [(5, 0), (10, 0)],
+        25: [(2, 0), (2, 1)],
+        26: [(5, 1), (10, 1)],
     }
 
-    def backward_step(u, _):
-        o = u // 2
-        c = 6 - o - (o + 3) // 7 + 2 * ((o + 2) // 7) - (o + 1) // 7
-
-        @pl.when(me >= nearest(c))
+    def unit(t, _):
+        for at, blocks in arrivals.items():
+            @pl.when(t == at)
+            def _(blocks=blocks):
+                for d, h in blocks:
+                    pass_on(d, h)
+
+        u = t - t // 14
+        c = u // 2
+
+        @pl.when(((t <= 12) | (t == 14)) & (me >= nearest(c)))
         def _():
-            backward(c, u % 2)
-
-        pl.when(u == 2)(write_attention)
+            forward(c, u % 2)
+
+        @pl.when(t == 1)
+        def _():
+            for h in range(KV):
+                send_own(1, h)
+
+        pl.when(t == 12)(lambda: finish(0))
+        pl.when(t == 14)(lambda: finish(1))
+
+        u2 = t - 14 + (27 - t) // 14
+        o = u2 // 2
+        c2 = 6 - o - (o + 4) // 7 + 3 * ((o + 2) // 7) - 2 * ((o + 1) // 7)
+
+        @pl.when(((t == 13) | (t >= 15)) & (me >= nearest(c2)))
+        def _():
+            backward(c2, u2 % 2)
+
+        pl.when(t == 19)(write_attention)
 
         for at, sums in leaving.items():
-            @pl.when(u == at)
+            @pl.when(t == at)
             def _(sums=sums):
                 for d, h in sums:
                     send_sum(d, h)
 
         return 0
 
-    lax.fori_loop(0, CHUNKS * KV, backward_step, 0)
-
-    for h in range(KV):
-        for j in range(TILES):
+    lax.fori_loop(0, UNITS, unit, 0)
+
+    rows = share.shape[1]
+
+    def put(row, sums):
+        share[row // rows, row % rows] = sums
+
+    lane = lax.broadcasted_iota(jnp.int32, (8, 2 * BLOCK), 1) // BLOCK
+    pick = (lane == lax.broadcasted_iota(jnp.int32, (8, 2 * BLOCK), 0)).astype(F32) * SCALE
+    for h in range(KV):
+        for j in range(TILES):
+            both = lax.dot_general(
+                pick, q_acc[h, j], (((1,), (1,)), ((), ())), precision=lax.Precision.HIGHEST, preferred_element_type=F32
+            )
             for e in range(2):
-                head = h * GROUP + j * 2 + e
-                grad = q_acc[h, j, :, e * 128:(e + 1) * 128].T * SCALE
-                share[head:head + 1, :] = jnp.sum(grad, axis=0, keepdims=True)
-                qg_out[:, head * 128:(head + 1) * 128] = grad.astype(BF16)
-        share[KV * GROUP + h:KV * GROUP + h + 1, :] = v_sum[h]
-
-    stores[1].start()
+                put(2 * (h * GROUP + j * 2 + e), both[e:e + 1])
+        put(2 * h + 1, v_sum[h])
 
     def ar_d(o):
-        return remote(share, share_d.at[o], ar_send.at[0, o], ar_recv.at[0, o], (d_peer(o), me, tp))
+        return remote(share.at[d_peer(o)], share_d.at[o], ar_send.at[0, o], ar_recv.at[0, o], (d_peer(o), me, tp))
 
     def ar_z(o):
         return remote(part, share_z.at[o], ar_send.at[1, o], ar_recv.at[1, o], (dp, z_peer(o), tp))
+
+    def ar_back(o):
+        return remote(sums.at[dp], sums.at[dp], ar_send.at[2, o], ar_recv.at[2, o], (d_peer(o), me, tp))
+
+    def ar_back_in(o):
+        source = lax.rem(dp + dps - o, dps)
+        return remote(sums.at[source], sums.at[source], ar_send.at[2, o], ar_recv.at[2, o], (d_peer(o), me, tp))
 
     def each(last, act):
         def body(o, _):
@@ -333,17 +354,26 @@
 
     each(dps, lambda o: ar_d(o).start())
     for h in range(KV):
+        for j in range(TILES):
+            for e in range(2):
+                at = (h * GROUP + j * 2 + e) * 128
+                qg_out[:, at:at + 128] = (q_acc[h, j, :, e * 128:(e + 1) * 128] * SCALE).astype(BF16).T
         send_sum(4, h)
         send_sum(11, h)
+    stores[1].start()
+    for h in range(KV):
+        send_sum(1, h)
     each(dps, lambda o: ar_d(o).wait_recv())
-    share_d[0] = share[...]
+    share_d[0] = share[dp]
     part[...] = jnp.sum(share_d[...], axis=0)
     farthest_first(lambda o: ar_z(o).start())
     for h in range(KV):
         send_sum(3, h)
         send_sum(12, h)
-    for h in range(KV):
-        send_sum(1, h)
+    each(RING, lambda o: ar_z(o).wait_recv())
+    share_z[0] = part[...]
+    sums[dp] = jnp.sum(share_z[...], axis=0) * (1.0 / dps)
+    each(dps, lambda o: ar_back(o).start())
 
     for h in range(KV):
         for d, into in ((1, 0), (3, 2), (12, 7)):
@@ -378,14 +408,16 @@
                     rs(d, h, n).wait_send()
     each(dps, lambda o: ar_d(o).wait_send())
 
-    each(RING, lambda o: ar_z(o).wait_recv())
-    share_z[0] = part[...]
-    sums = jnp.sum(share_z[...], axis=0) * (1.0 / dps)
-    qbg_ref[...] = sums[:KV * GROUP]
-    vbg_ref[...] = sums[KV * GROUP:KV * GROUP + KV]
+    each(dps, lambda o: ar_back_in(o).wait_recv())
+    for row in range(2 * KV * GROUP):
+        if row % 2 == 0:
+            qbg_ref[row // 2:row // 2 + 1, :] = sums[row // rows, row % rows]
+        elif row < 2 * KV:
+            vbg_ref[row // 2:row // 2 + 1, :] = sums[row // rows, row % rows]
     stores[4].start()
     stores[5].start()
     each(RING, lambda o: ar_z(o).wait_send())
+    each(dps, lambda o: ar_back(o).wait_send())
     for copy in stores:
         copy.wait()
 
@@ -455,18 +487,19 @@
             pltpu.VMEM((KV, 1, HEAD_DIM), F32),
             pltpu.VMEM((13,) + block, BF16),
             pltpu.VMEM((13,) + block, BF16),
-            pltpu.VMEM((ROWS, HEAD_DIM), F32),
-            pltpu.VMEM((dps, ROWS, HEAD_DIM), F32),
-            pltpu.VMEM((ROWS, HEAD_DIM), F32),
-            pltpu.VMEM((RING, ROWS, HEAD_DIM), F32),
+            pltpu.VMEM((dps, ROWS // dps, 1, HEAD_DIM), F32),
+            pltpu.VMEM((dps, ROWS // dps, 1, HEAD_DIM), F32),
+            pltpu.VMEM((ROWS // dps, 1, HEAD_DIM), F32),
+            pltpu.VMEM((RING, ROWS // dps, 1, HEAD_DIM), F32),
+            pltpu.VMEM((dps, ROWS // dps, 1, HEAD_DIM), F32),
             pltpu.SemaphoreType.DMA((7,)),
             pltpu.SemaphoreType.DMA((6,)),
             pltpu.SemaphoreType.DMA((13, KV, 2)),
             pltpu.SemaphoreType.DMA((13, KV, 2)),
             pltpu.SemaphoreType.DMA((13, KV, 2)),
             pltpu.SemaphoreType.DMA((13, KV, 2)),
-            pltpu.SemaphoreType.DMA((2, RING)),
-            pltpu.SemaphoreType.DMA((2, RING)),
+            pltpu.SemaphoreType.DMA((3, RING)),
+            pltpu.SemaphoreType.DMA((3, RING)),
         ],
         compiler_params=pltpu.CompilerParams(
             collective_id=0, has_side_effects=True, vmem_limit_bytes=60 * 2**20

time: 88.6 us -> 85.7 us (0.967)
  the two profiles are of different devices: /device:TPU:64 before, /device:TPU:32 now
where the time goes in v4:
time: 85.7 us; the launch traced here: 85.5 us
  Pallas kernels  84.8 us (99%)
    pallas_call x1, Pallas kernels, shards(): pl.pallas_call(kernel, out_shape=results, in_specs=[hbm] * 7, out_specs=(...  82.5 us
    pallas_call x1, Pallas kernels, shards(): pl.pallas_call(write_out, out_shape=results, in_specs=[hbm] * 6, out_spec...  2.3 us

profile of v4, /device:TPU:32, one launch (start us, length us, event | category | flops | bytes accessed | tf_op | source)
XLA Modules:
  0.0 85.5 jit_solution(12384212620270465817)
XLA Ops:
  0.6 82.5 %attention.1 = (bf16[128,2048]{1,0:T(8,128)(2,1)}, bf16[128,2048]{1,0:T(8,128)(2,1)}, bf16[128,256]{1,0:T(8,128)(2,1)}, bf16[128,256]{1,0:T(8,128)(2,1)}, f32[16,128]{1,0:T(8,128)}, /*index=5*/f32[2,128]{1,0:T(2,128)}) custom-call(bf16[128,2048]{1,0:T(8,128)(2,1)} %bitcast.12, bf16[16,128]{1,0:T(8,128)(2,1)} %bitcast.21, bf16[128,256]{1,0:T(8,128)(2,1)} %bitcast.16, ...), custom_call_target="tpu_custom_call" | custom-call | flops 6000000000 | bytes 3000000 | tf_op jit(solution)/shard_map/attention/pallas_call | solution.py:458
  83.2 2.3 %write_out.1 = (bf16[128,2048]{1,0:T(8,128)(2,1)}, bf16[128,2048]{1,0:T(8,128)(2,1)}, bf16[128,256]{1,0:T(8,128)(2,1)}, bf16[128,256]{1,0:T(8,128)(2,1)}, f32[16,128]{1,0:T(8,128)}, /*index=5*/f32[2,128]{1,0:T(2,128)}) custom-call(bf16[128,2048]{1,0:T(8,128)(2,1)} %get-tuple-element.18.refs_0_, bf16[128,2048]{1,0:T(8,128)(2,1)} %get-tuple-element.19.refs_1_, ...), custom_call_target="tpu_custom_call" | custom-call | tf_op jit(solution)/shard_map/write_out/pallas_call | solution.py:518

commit v5 on v4

--- a/solution.py
+++ b/solution.py
@@ -56,7 +56,7 @@
         for i, (src, dst) in enumerate((
             (k_hbm, k_in), (v_hbm, v_in), (vb_hbm, vb_in), (q_hbm, q_in), (g_hbm, g_in), (qb_hbm, qb_in), (len_hbm, lens)))
     ]
-    for copy in loads:
+    for copy in loads[:3]:
         copy.start()
 
     stores = [
@@ -74,6 +74,8 @@
         return 0
 
     lax.fori_loop(1, dps, greet_d, 0)
+    for copy in loads[3:]:
+        copy.start()
 
     def remote(src, dst, send, recv, device):
         return pltpu.make_async_remote_copy(
@@ -97,7 +99,6 @@
         kv[0, h, 0] = k_in[:, cols]
         kv[0, h, 1] = (v_in[:, cols].astype(F32) + vb_in[h:h + 1, :].astype(F32)).astype(BF16)
     nothing = jnp.zeros((KV, 2, BLOCK, HEAD_DIM), BF16)
-    kv[1] = nothing
     pl.semaphore_wait(barrier, len(STEPS) + dps - 1)
 
     def send_own(to, h):
@@ -143,23 +144,24 @@
         end = end + lens[0, d]
         begin = jnp.where(position >= end, end, begin)
 
-    def forward(c, h):
+    def forward(c, h, count):
         near = nearest(c)
         far = jnp.where(c == 0, -1, jnp.where(c == 3, 2, jnp.where(c <= 2, 13 - c, 14 - c)))
         offset = lax.broadcasted_iota(jnp.int32, (BLOCK, BLOCK), 0)
         bias = []
-        for d in (near, far):
+        for d in (near, far)[:count]:
             at = (me - d) * BLOCK + offset
             bias.append(jnp.where((at >= begin) & (at <= position), 0.0, NEG).astype(F32))
         bias = jnp.concatenate(bias, axis=0)
-        pair = kv[pl.ds(2 * c, 2), h]
-        keys = pair[:, 0].reshape(2 * BLOCK, HEAD_DIM)
-        values_t = pair[:, 1].reshape(2 * BLOCK, HEAD_DIM).T
+        size = count * BLOCK
+        pair = kv[pl.ds(2 * c, count), h]
+        keys = pair[:, 0].reshape(size, HEAD_DIM)
+        values_t = pair[:, 1].reshape(size, HEAD_DIM).T
         for j in range(TILES):
             for e in range(2):
                 at = slice(e * 128, (e + 1) * 128)
                 score = jnp.dot(keys, q_cols[h, j, :, at], preferred_element_type=F32) * (SCALE * LOG2E) + bias
-                scores[c, h, j, :, at] = score
+                scores[c, h, j, :size, at] = score
                 old = top[h, j, :, at]
                 new = jnp.maximum(old, jnp.max(score, axis=0, keepdims=True))
                 fade = jnp.exp2(old - new)
@@ -199,23 +201,24 @@
                     attn_out[:, at:at + 128] = attn_t[h, j, :, e * 128:(e + 1) * 128].T
         stores[0].start()
 
-    def backward(c, h):
-        pair = kv[pl.ds(2 * c, 2), h]
-        keys_t = pair[:, 0].reshape(2 * BLOCK, HEAD_DIM).T
-        values = pair[:, 1].reshape(2 * BLOCK, HEAD_DIM)
+    def backward(c, h, count):
+        size = count * BLOCK
+        pair = kv[pl.ds(2 * c, count), h]
+        keys_t = pair[:, 0].reshape(size, HEAD_DIM).T
+        values = pair[:, 1].reshape(size, HEAD_DIM)
         for j in range(TILES):
             at = slice(j * 256, (j + 1) * 256)
-            probs = jnp.exp2(scores[c, h, j] - top[h, j])
+            probs = jnp.exp2(scores[c, h, j, :size] - top[h, j])
             dprob = jnp.dot(values, g_cols[h, j], preferred_element_type=F32)
-            dscores[:, at] = (probs * (dprob - delta[h, j])).astype(BF16)
-            probs_b[:, at] = probs.astype(BF16)
-        v_term = jnp.dot(probs_b[...], g_rows[h].reshape(GROUP * BLOCK, HEAD_DIM), preferred_element_type=F32)
-        k_term = jnp.dot(dscores[...], q_rows[h].reshape(GROUP * BLOCK, HEAD_DIM), preferred_element_type=F32)
-        q_term = jnp.dot(keys_t, dscores[...], preferred_element_type=F32)
+            dscores[:size, at] = (probs * (dprob - delta[h, j])).astype(BF16)
+            probs_b[:size, at] = probs.astype(BF16)
+        v_term = jnp.dot(probs_b[:size], g_rows[h].reshape(GROUP * BLOCK, HEAD_DIM), preferred_element_type=F32)
+        k_term = jnp.dot(dscores[:size], q_rows[h].reshape(GROUP * BLOCK, HEAD_DIM), preferred_element_type=F32)
+        q_term = jnp.dot(keys_t, dscores[:size], preferred_element_type=F32)
         for j in range(TILES):
             q_acc[h, j] += q_term[:, j * 256:(j + 1) * 256]
-        terms[pl.ds(2 * c, 2), h, 0] = (k_term * SCALE).reshape(2, BLOCK, HEAD_DIM)
-        terms[pl.ds(2 * c, 2), h, 1] = v_term.reshape(2, BLOCK, HEAD_DIM)
+        terms[pl.ds(2 * c, count), h, 0] = (k_term * SCALE).reshape(count, BLOCK, HEAD_DIM)
+        terms[pl.ds(2 * c, count), h, 1] = v_term.reshape(count, BLOCK, HEAD_DIM)
         v_sum[h] += jnp.sum(v_term, axis=0, keepdims=True)
 
     def rs(d, h, n):
@@ -277,9 +280,13 @@
         u = t - t // 14
         c = u // 2
 
-        @pl.when(((t <= 12) | (t == 14)) & (me >= nearest(c)))
-        def _():
-            forward(c, u % 2)
+        @pl.when(t < 2)
+        def _():
+            forward(0, t, 1)
+
+        @pl.when((((t >= 2) & (t <= 12)) | (t == 14)) & (me >= nearest(c)))
+        def _():
+            forward(c, u % 2, 2)
 
         @pl.when(t == 1)
         def _():
@@ -293,11 +300,13 @@
         o = u2 // 2
         c2 = 6 - o - (o + 4) // 7 + 3 * ((o + 2) // 7) - 2 * ((o + 1) // 7)
 
-        @pl.when(((t == 13) | (t >= 15)) & (me >= nearest(c2)))
-        def _():
-            backward(c2, u2 % 2)
-
-        pl.when(t == 19)(write_attention)
+        @pl.when(((t == 13) | (t >= 15)) & (t < 26) & (me >= nearest(c2)))
+        def _():
+            backward(c2, u2 % 2, 2)
+
+        @pl.when(t >= 26)
+        def _():
+            backward(0, u2 % 2, 1)
 
         for at, sums in leaving.items():
             @pl.when(t == at)
@@ -353,16 +362,9 @@
         lax.fori_loop(0, RING - 1, body, 0)
 
     each(dps, lambda o: ar_d(o).start())
-    for h in range(KV):
-        for j in range(TILES):
-            for e in range(2):
-                at = (h * GROUP + j * 2 + e) * 128
-                qg_out[:, at:at + 128] = (q_acc[h, j, :, e * 128:(e + 1) * 128] * SCALE).astype(BF16).T
-        send_sum(4, h)
-        send_sum(11, h)
-    stores[1].start()
-    for h in range(KV):
-        send_sum(1, h)
+    for d in (4, 11, 1):
+        for h in range(KV):
+            send_sum(d, h)
     each(dps, lambda o: ar_d(o).wait_recv())
     share_d[0] = share[dp]
     part[...] = jnp.sum(share_d[...], axis=0)
@@ -370,6 +372,14 @@
     for h in range(KV):
         send_sum(3, h)
         send_sum(12, h)
+
+    write_attention()
+    for h in range(KV):
+        for j in range(TILES):
+            for e in range(2):
+                at = (h * GROUP + j * 2 + e) * 128
+                qg_out[:, at:at + 128] = (q_acc[h, j, :, e * 128:(e + 1) * 128] * SCALE).astype(BF16).T
+    stores[1].start()
     each(RING, lambda o: ar_z(o).wait_recv())
     share_z[0] = part[...]
     sums[dp] = jnp.sum(share_z[...], axis=0) * (1.0 / dps)

time: 85.7 us -> 85.1 us (level)
  no operation moved by 1% of the time
where the time goes in v5:
time: 85.1 us; the launch traced here: 84.9 us
  Pallas kernels  84.3 us (99%)
    pallas_call x1, Pallas kernels, shards(): pl.pallas_call(kernel, out_shape=results, in_specs=[hbm] * 7, out_specs=(...  82 us
    pallas_call x1, Pallas kernels, shards(): pl.pallas_call(write_out, out_shape=results, in_specs=[hbm] * 6, out_spec...  2.3 us

profile of v5, /device:TPU:32, one launch (start us, length us, event | category | flops | bytes accessed | tf_op | source)
XLA Modules:
  0.0 84.9 jit_solution(14857520769820963760)
XLA Ops:
  0.6 82.0 %attention.1 = (bf16[128,2048]{1,0:T(8,128)(2,1)}, bf16[128,2048]{1,0:T(8,128)(2,1)}, bf16[128,256]{1,0:T(8,128)(2,1)}, bf16[128,256]{1,0:T(8,128)(2,1)}, f32[16,128]{1,0:T(8,128)}, /*index=5*/f32[2,128]{1,0:T(2,128)}) custom-call(bf16[128,2048]{1,0:T(8,128)(2,1)} %bitcast.12, bf16[16,128]{1,0:T(8,128)(2,1)} %bitcast.21, bf16[128,256]{1,0:T(8,128)(2,1)} %bitcast.16, ...), custom_call_target="tpu_custom_call" | custom-call | flops 6000000000 | bytes 3000000 | tf_op jit(solution)/shard_map/attention/pallas_call | solution.py:468
  82.6 2.3 %write_out.1 = (bf16[128,2048]{1,0:T(8,128)(2,1)}, bf16[128,2048]{1,0:T(8,128)(2,1)}, bf16[128,256]{1,0:T(8,128)(2,1)}, bf16[128,256]{1,0:T(8,128)(2,1)}, f32[16,128]{1,0:T(8,128)}, /*index=5*/f32[2,128]{1,0:T(2,128)}) custom-call(bf16[128,2048]{1,0:T(8,128)(2,1)} %get-tuple-element.18.refs_0_, bf16[128,2048]{1,0:T(8,128)(2,1)} %get-tuple-element.19.refs_1_, ...), custom_call_target="tpu_custom_call" | custom-call | tf_op jit(solution)/shard_map/write_out/pallas_call | solution.py:528
